TPU v7x, 256 devices: a whole 4x4x8 slice. The times are simulated.
256 devices in a mesh: dp: 32 (over z_lo, x, core), mp: 8 (over y, z_hi).
Axes of the slice: x: 4, y: 4, z: 8 (z_hi: 2, z_lo: 4; z = z_hi * 4 + z_lo), core: 2. Of those that a mesh axis runs over, the one named last changes fastest.
Arguments:
- attn_out: bfloat16 [2, 4096, 4096], P(None, 'dp', 'mp'), may hold values from -24 to 24
- residual: bfloat16 [2, 4096, 4096], P(None, 'dp', 'mp'), may hold values from -24 to 24
- o_weight: bfloat16 [4096, 4096], P('mp'), may hold values from -0.09375 to 0.09375
- norm_gain: float32 [4096], P('mp'), may hold values from 0.1 to 1.9
- positive: int32 [4096], P('dp'), may hold values from 0 to 4095, each once
Outputs:
- pair_loss: float32 [4096], P('dp')
- resid_grad: float32 [2, 4096, 4096], P(None, 'dp', 'mp')
- attn_grad: float32 [2, 4096, 4096], P(None, 'dp', 'mp')
- weight_grad: float32 [4096, 4096], P('mp', 'dp')
Inputs may be any that keep to these rules, and one draw needn't show every extreme that they name: Each response is the positive of exactly one query.
All inputs are finite; a program needn't handle non-finite values.
Results may differ from a plain program's by a relative error of at most 0.0041.
Values may be sent and summed in bfloat16 or wider, within the bound.
A program may use at most 64 MiB of HBM per device.

v0:
```python
import jax
import jax.numpy as jnp
from jax import lax
from jax.sharding import PartitionSpec as P

LOGIT_SCALE = 50.0
EPS = 1e-06


def body(attn_out, residual, o_weight, norm_gain, positive):
    halves, local_pairs, shard_width = attn_out.shape
    total_pairs = local_pairs * lax.axis_size("dp")
    attn_rows = attn_out.reshape(halves * local_pairs, shard_width)
    partial_value = jnp.dot(attn_rows, o_weight, preferred_element_type=jnp.float32)
    projected = lax.psum_scatter(partial_value, "mp", scatter_dimension=1, tiled=True)
    scaled = (
        residual.reshape(halves * local_pairs, shard_width).astype(jnp.float32) + projected
    ) * norm_gain
    squares = lax.psum(jnp.sum(scaled * scaled, axis=1), "mp")
    inverse = lax.rsqrt(squares + EPS)
    embedded = (scaled * inverse[:, None]).astype(jnp.bfloat16)
    queries = embedded[:local_pairs]
    answers = embedded[local_pairs:]
    all_answers = lax.all_gather(answers, "dp", axis=0, tiled=True)
    partial_scores = lax.dot_general(
        queries, all_answers, (((1,), (1,)), ((), ())), preferred_element_type=jnp.float32
    )
    logits = LOGIT_SCALE * lax.psum(partial_scores, "mp")
    row_top = jnp.max(logits, axis=1)
    log_total = row_top + jnp.log(jnp.sum(jnp.exp(logits - row_top[:, None]), axis=1))
    is_positive = positive[:, None] == jnp.arange(total_pairs, dtype=jnp.int32)[None, :]
    pair_loss = log_total - jnp.sum(jnp.where(is_positive, logits, 0.0), axis=1)
    score_grad = (
        LOGIT_SCALE * (jnp.exp(logits - log_total[:, None]) - is_positive.astype(jnp.float32))
    ).astype(jnp.bfloat16)
    grad_queries = jnp.dot(score_grad, all_answers, preferred_element_type=jnp.float32)
    block = score_grad
    grad_answers = lax.psum_scatter(
        lax.dot_general(
            block, queries, (((0,), (0,)), ((), ())), preferred_element_type=jnp.float32
        ),
        "dp",
        scatter_dimension=0,
        tiled=True,
    )
    grad_embedded = jnp.concatenate([grad_queries, grad_answers], axis=0)
    radial = lax.psum(jnp.sum(grad_embedded * scaled, axis=1), "mp")
    grad_scaled = (
        inverse[:, None] * grad_embedded - (inverse * inverse * inverse * radial)[:, None] * scaled
    )
    resid_grad = norm_gain * grad_scaled
    grad_wire = resid_grad.astype(jnp.bfloat16)
    block = lax.all_gather(grad_wire, "mp", axis=1, tiled=True)
    back = lax.dot_general(
        block, o_weight, (((1,), (1,)), ((), ())), preferred_element_type=jnp.float32
    )
    weight_block = lax.dot_general(
        attn_rows, block, (((0,), (0,)), ((), ())), preferred_element_type=jnp.float32
    )
    weight_grad = lax.psum_scatter(weight_block, "dp", scatter_dimension=1, tiled=True)
    return (
        pair_loss,
        resid_grad.reshape(halves, local_pairs, shard_width),
        back.reshape(halves, local_pairs, shard_width),
        weight_grad,
    )


def solution(mesh):
    placed = (P(None, "dp", "mp"), P(None, "dp", "mp"), P("mp", None), P("mp"), P("dp"))
    return jax.shard_map(
        body,
        mesh=mesh,
        in_specs=placed,
        out_specs=(P("dp"), P(None, "dp", "mp"), P(None, "dp", "mp"), P("mp", "dp")),
        check_vma=False,
    )
```

profile of v0, /device:TPU:8, one launch (start us, length us, event | category | flops | bytes accessed | tf_op | source)
XLA Modules:
  0.0 863.5 jit_solution(2259598796366238865)
XLA Ops:
  7.2 0.0 copy-start
  7.2 0.0 reduce-scatter.4.cloned.1.call-start
  7.2 0.9 copy-done
  8.1 5.4 fusion.9
  13.5 0.0 copy-start.3
  13.5 0.0 copy-start.5
  13.5 0.0 reduce-scatter.4.cloned.1.call-update
  13.5 0.0 all-gather.3.cloned.1.call-start
  13.6 130.1 %reduce-scatter.4.cloned.1.call-done = f32[256,512]{1,0:T(8,128)} async-done(((f32[256,4096]{1,0:T(8,128)}), f32[256,512]{1,0:T(8,128)}) %reduce-scatter.4.cloned.1.call-update) | async-done | bytes 524304 | tf_op jit(solution)/shard_map/reduce_scatter | solution.py:15
  143.7 0.0 copy-done.3
  143.7 0.0 copy-done.5
  143.7 1.2 multiply_reduce_fusion.2
  144.9 22.0 %psum.21 = f32[256]{0:T(256)S(1)} all-reduce(f32[256]{0:T(256)S(1)} %multiply_reduce_fusion.2), channel_id=1, replica_groups=mesh['dp'=32,'mp'=8] {'mp'}, use_global_device_ids=true, to_apply=%region_2.0 | all-reduce | flops 256 | bytes 2048 | tf_op jit(solution)/shard_map/psum | solution.py:19
  166.9 1.1 multiply_convert_fusion.1
  168.1 0.7 slice.9
  168.7 0.0 all-gather.3.cloned.1.call-update
  168.8 0.0 all-reduce.2.cloned.1.call-start
  168.8 64.1 %all-gather.3.cloned.1.call-done = bf16[4096,512]{1,0:T(8,128)(2,1)} async-done(((bf16[128,512]{1,0:T(8,128)(2,1)}), bf16[4096,512]{1,0:T(8,128)(2,1)}) %all-gather.3.cloned.1.call-update) | async-done | bytes 4194320 | tf_op jit(solution)/shard_map/all_gather | solution.py:24
  232.9 5.0 fusion.3
  237.9 0.0 copy-start.6
  237.9 0.0 all-reduce.2.cloned.1.call-update
  237.9 0.0 reduce-scatter.6.cloned.1.call-start
  238.0 191.7 %all-reduce.2.cloned.1.call-done = f32[128,4096]{1,0:T(8,128)} async-done(((f32[128,4096]{1,0:T(8,128)}), f32[128,4096]{1,0:T(8,128)}) %all-reduce.2.cloned.1.call-update) | async-done | bytes 2097168 | tf_op jit(solution)/shard_map/psum | solution.py:28
  429.7 0.0 copy-start.1
  429.7 2.0 multiply_reduce_fusion
  431.7 0.0 copy-done.6
  431.7 0.3 copy-done.1
  431.9 0.8 select_reduce_fusion
  432.7 0.5 fusion.8
  433.2 4.7 fusion.1
  437.9 0.0 reduce-scatter.6.cloned.1.call-update
  438.0 0.0 copy-start.2
  438.0 0.0 all-gather.5.cloned.1.call-start
  438.0 3.2 fusion.6
  441.2 153.5 %reduce-scatter.6.cloned.1.call-done = f32[128,512]{1,0:T(8,128)} async-done(((f32[4096,512]{1,0:T(8,128)}), f32[128,512]{1,0:T(8,128)}) %reduce-scatter.6.cloned.1.call-update) | async-done | bytes 262160 | tf_op jit(solution)/shard_map/reduce_scatter | solution.py:38
  594.7 0.0 copy-done.2
  594.7 1.1 multiply_reduce_fusion.1
  595.8 26.9 %psum.23 = f32[256]{0:T(256)S(1)} all-reduce(f32[256]{0:T(256)S(1)} %multiply_reduce_fusion.1), channel_id=1, replica_groups=mesh['dp'=32,'mp'=8] {'mp'}, use_global_device_ids=true, to_apply=%region_9.10 | all-reduce | flops 256 | bytes 2048 | tf_op jit(solution)/shard_map/psum | solution.py:47
  622.7 2.0 fusion.7
  624.7 0.0 all-gather.5.cloned.1.call-update
  624.7 0.0 reduce-scatter.8.cloned.1.call-start
  624.8 70.2 %all-gather.5.cloned.1.call-done = bf16[256,4096]{1,0:T(8,128)(2,1)} async-done(((bf16[256,512]{1,0:T(8,128)(2,1)}), bf16[256,4096]{1,0:T(8,128)(2,1)}) %all-gather.5.cloned.1.call-update) | async-done | bytes 2097168 | tf_op jit(solution)/shard_map/all_gather | solution.py:53
  695.0 6.1 convolution_bitcast_fusion
  701.1 0.0 reduce-scatter.8.cloned.1.call-update
  701.1 1.6 copy-done.4
  702.6 4.3 fusion.10
  706.9 148.0 %reduce-scatter.8.cloned.1.call-done = f32[512,128]{0,1:T(8,128)} async-done(((f32[512,4096]{0,1:T(8,128)}), f32[512,128]{0,1:T(8,128)}) %reduce-scatter.8.cloned.1.call-update) | async-done | bytes 262160 | tf_op jit(solution)/shard_map/reduce_scatter | solution.py:60
  854.9 1.8 copy.9
  (3 shorter events, 0.0 us)
Async XLA Ops:
  7.2 1.0 copy-start
  7.2 136.5 %reduce-scatter.4.cloned.1.call-start = ((), (), s32[]{:S(2)}) async-start(), calls=%async_computation.3 | async-start | bytes 4718592 | tf_op jit(solution)/shard_map/reduce_scatter | solution.py:15
  13.5 130.2 %copy-start.3 = (bf16[2,128,512]{2,1,0:T(8,128)(2,1)S(1)}, bf16[2,128,512]{2,1,0:T(8,128)(2,1)}, u32[]{:S(2)}) copy-start(bf16[2,128,512]{2,1,0:T(8,128)(2,1)} %param.6) | copy-start | bytes 786436
  13.5 130.2 %copy-start.5 = (f32[512]{0:T(512)S(1)}, f32[512]{0:T(512)}, u32[]{:S(2)}) copy-start(f32[512]{0:T(512)} %param.8) | copy-start | bytes 6148
  13.5 219.4 %all-gather.3.cloned.1.call-start = ((), (), s32[]{:S(2)}) async-start(), calls=%async_computation.4 | async-start | bytes 4325376 | tf_op jit(solution)/shard_map/all_gather | solution.py:24
  168.8 261.0 %all-reduce.2.cloned.1.call-start = ((), (), s32[]{:S(2)}) async-start(), calls=%async_computation.5 | async-start | bytes 4194304 | tf_op jit(solution)/shard_map/psum | solution.py:28
  237.9 193.8 %copy-start.6 = (s32[128]{0:T(128)S(1)}, s32[128]{0:T(128)}, u32[]{:S(2)}) copy-start(s32[128]{0:T(128)} %param.9) | copy-start | bytes 1540
  237.9 356.7 %reduce-scatter.6.cloned.1.call-start = ((), (), s32[]{:S(2)}) async-start(), calls=%async_computation.6 | async-start | bytes 8650752 | tf_op jit(solution)/shard_map/reduce_scatter | solution.py:38
  429.7 2.2 copy-start.1
  438.0 156.7 %copy-start.2 = (f32[256,512]{1,0:T(8,128)S(1)}, f32[256,512]{1,0:T(8,128)}, u32[]{:S(2)}) copy-start(f32[256,512]{1,0:T(8,128)} %reduce-scatter.4.cloned.1.call-done) | copy-start | bytes 1572868
  438.0 257.0 %all-gather.5.cloned.1.call-start = ((), (), s32[]{:S(2)}) async-start(), calls=%async_computation.7 | async-start | bytes 2359296 | tf_op jit(solution)/shard_map/all_gather | solution.py:53
  624.7 230.2 %reduce-scatter.8.cloned.1.call-start = ((), (), s32[]{:S(2)}) async-start(), calls=%async_computation.8 | async-start | bytes 8650752 | tf_op jit(solution)/shard_map/reduce_scatter | solution.py:60
  701.1 1.6 copy-start.4
Sparse Core Ops, SparseCore 0:
  13.6 129.9 reduce-scatter.3
  168.9 64.0 all-gather.2
  238.0 191.6 all-reduce.1
  438.1 156.5 reduce-scatter.5
  624.8 70.0 all-gather.4
  701.2 153.6 reduce-scatter.7
where the time goes:
time: 864 us
  waiting for transfers between devices  758 us (88%)
  blocking collectives  48.9 us (6%)
  matrix products  28.6 us (3%)
  between operations  14.1 us (2%)
  other arithmetic  8.76 us (1%)
    psum x1, waiting for transfers between devices, body(): logits = LOGIT_SCALE * lax.psum(partial_scores, 'mp')  192 us
    reduce_scatter x1, waiting for transfers between devices, body(): lax.psum_scatter(lax.dot_general(block, queries, (((0,), (0,)), ((), ()))...  153 us
    reduce_scatter x1, waiting for transfers between devices, body(): lax.psum_scatter(weight_block, 'dp', scatter_dimension=1, tiled=True)  148 us
    reduce_scatter x1, waiting for transfers between devices, body(): lax.psum_scatter(partial_value, 'mp', scatter_dimension=1, tiled=True)  130 us
    all_gather x1, waiting for transfers between devices, body(): block = lax.all_gather(grad_wire, 'mp', axis=1, tiled=True)  70.2 us
    all_gather x1, waiting for transfers between devices, body(): all_answers = lax.all_gather(answers, 'dp', axis=0, tiled=True)  64.1 us
    psum x1, blocking collectives, body(): radial = lax.psum(jnp.sum(grad_embedded * scaled, axis=1), 'mp')  26.9 us
    psum x1, blocking collectives, body(): squares = lax.psum(jnp.sum(scaled * scaled, axis=1), 'mp')  22 us
  transfers between devices with their start and end apart: 6, of which 6 were waited for; matrix products, arithmetic and copies ran while one was open for 1% of the time, Pallas kernels for 0%

commit v1 on v0

v1 whole, which is shorter than its diff:
```python
import jax
import jax.numpy as jnp
from jax import lax
from jax.sharding import PartitionSpec as P
from jax.experimental import pallas as pl
from jax.experimental.pallas import tpu as pltpu

LOGIT_SCALE = 50.0
EPS = 1e-06
F32 = jnp.float32
BF16 = jnp.bfloat16
MESH = pl.DeviceIdType.MESH
WIRE = BF16

STAGES = dict(
    y1=6, z1=1, ss=7, qx=3, ps=3, ax=3, az=3, ac=4, ly=6, lz=1, tx=3, pl=7,
    sz=1, sy=6, gc=4, gz=3, gq=3, rq=7, ra=7, gh=2, gy=12, gx=24, wc=4, wz=3,
)
BASE = {}
COUNT = 0
for _name, _n in STAGES.items():
    BASE[_name] = COUNT
    COUNT += _n


def nt(a, b):
    return lax.dot_general(a, b, (((1,), (1,)), ((), ())), preferred_element_type=F32)


def tn(a, b):
    return lax.dot_general(a, b, (((0,), (0,)), ((), ())), preferred_element_type=F32)


def nn(a, b):
    return lax.dot_general(a, b, (((1,), (0,)), ((), ())), preferred_element_type=F32)


def to_row(col):
    n = col.shape[0]
    return jnp.broadcast_to(col, (n, 128)).T[0:8]


def to_col(row):
    n = row.shape[1]
    return jnp.broadcast_to(row, (128, n)).T[:, 0:1]


def rows(start, size, unit=None):
    return pl.ds(pl.multiple_of(start, unit or size), size)


def kernel(
    a_ref, r_ref, w_ref, gain_ref, pos_ref,
    loss_ref, rg_ref, ag_ref, wg_ref,
    ys, yr, own, zs, zr, sc, inv_s, ssb,
    qx, aa, px, pt, lg, lr, lzs, lzr, eb, txb, lossb,
    sa, gap, gcr, gzs, gzr, gqs, gqr, ge, rb,
    gg, gx, ax, tb, tcr, wzs, wzr,
    send, recv,
):
    dp = lax.axis_index("dp")
    mp = lax.axis_index("mp")
    core, x, zl = dp % 2, (dp // 2) % 4, dp // 8
    y, zh = mp // 2, mp % 2
    j = mp
    pending = []

    def dev(core=core, x=x, zl=zl, y=y, zh=zh):
        return ((zl * 4 + x) * 2 + core, y * 2 + zh)

    def copy(stage, k, src, dst, to):
        return pltpu.make_async_remote_copy(
            src_ref=src, dst_ref=dst,
            send_sem=send.at[BASE[stage] + k], recv_sem=recv.at[BASE[stage] + k],
            device_id=to, device_id_type=MESH,
        )

    def go(*args):
        c = copy(*args)
        c.start()
        pending.append(c)

    def got(stage, k, dst):
        copy(stage, k, dst, dst, dev(core=1 - core)).wait_recv()

    def ring(v, d):
        return (v + d) % 4

    others = [(d, e) for d in (2, 1, 3, 0) for e in (1, 0) if (d, e) != (0, 0)]

    barrier = pltpu.get_barrier_semaphore()
    peers = [dev(y=ring(y, d), zh=(zh + e) % 2) for d, e in others]
    peers += [dev(x=ring(x, d)) for d in (1, 2, 3)]
    peers += [dev(zl=ring(zl, d)) for d in (1, 2, 3)]
    peers += [dev(core=1 - core)]
    for p in peers:
        pl.semaphore_signal(barrier, inc=1, device_id=p, device_id_type=MESH)

    def wcols(yy, e):
        return w_ref[:, rows(yy * 1024 + e * 512, 512)]

    for er in (0, 1):
        e = (1 - zh) if er == 0 else zh
        for d in (2, 1, 3):
            ys[er * 3 + d - 1] = nn(a_ref[...], wcols(ring(y, d), e)).astype(WIRE)
    px[x] = jnp.broadcast_to(pos_ref[...], (8, 128))
    pl.semaphore_wait(barrier, len(peers))
    for er in (0, 1):
        for d in (2, 1, 3):
            s = er * 3 + d - 1
            go("y1", s, ys.at[s], yr.at[s], dev(y=ring(y, d)))
    for d in (2, 1, 3):
        go("ps", d - 1, px.at[x], px.at[x], dev(x=ring(x, d)))
        go("ax", d - 1, a_ref, ax.at[rows(x * 256, 256)], dev(x=ring(x, d)))
    ax[rows(x * 256, 256), :] = a_ref[...]
    own[0] = nn(a_ref[...], wcols(y, 1 - zh))
    own[1] = nn(a_ref[...], wcols(y, zh))
    for d in (1, 3, 2):
        got("y1", d - 1, yr.at[d - 1])
    zs[...] = (
        own[0] + yr[0].astype(F32) + yr[1].astype(F32) + yr[2].astype(F32)
    ).astype(WIRE)
    go("z1", 0, zs, zr, dev(zh=1 - zh))
    for d in (1, 3, 2):
        got("y1", 3 + d - 1, yr.at[3 + d - 1])
    own[1] = own[1] + yr[3].astype(F32) + yr[4].astype(F32) + yr[5].astype(F32)
    got("z1", 0, zr)
    scaled = (r_ref[...].astype(F32) + (own[1] + zr[...].astype(F32))) * gain_ref[...]
    sc[...] = scaled

    ssb[0] = to_row(jnp.sum(scaled * scaled, axis=1, keepdims=True))
    for d, e in others:
        k = d * 2 + e
        go("ss", k - 1, ssb.at[0], ssb.at[k], dev(y=ring(y, d), zh=(zh + e) % 2))
    for d, e in others[::-1]:
        k = d * 2 + e
        got("ss", k - 1, ssb.at[k])
    total = ssb[0]
    for k in range(1, 8):
        total = total + ssb[k]
    inv = to_col(lax.rsqrt(total[0:1] + EPS))
    inv_s[...] = jnp.broadcast_to(inv, (256, 128))

    emb = (sc[...] * inv).astype(BF16)
    a_at = rows((zl * 2 + core) * 128, 128)
    aa[a_at, :] = emb[128:256]
    for d in (2, 1, 3):
        go("az", d - 1, aa.at[a_at], aa.at[a_at], dev(zl=ring(zl, d)))
    q_at = rows(x * 128, 128)
    qx[q_at, :] = emb[0:128]
    for d in (2, 1, 3):
        go("qx", d - 1, qx.at[q_at], qx.at[q_at], dev(x=ring(x, d)))
    go("ac", 0, aa.at[a_at], aa.at[a_at], dev(core=1 - core))
    for d in (1, 3, 2):
        got("qx", d - 1, qx.at[rows(ring(x, -d) * 128, 128)])

    for t in (0, 1, 3, 2):
        zz = ring(zl, -t)
        if t:
            at = rows((zz * 2 + core) * 128, 128)
            got("az", t - 1, aa.at[at])
            go("ac", t, aa.at[at], aa.at[at], dev(core=1 - core))
        got("ac", t, aa.at[rows((zz * 2 + 1 - core) * 128, 128)])
        lg[:, rows(zz * 256, 256)] = nt(qx[...], aa[rows(zz * 256, 256), :])

    def block(yy, e):
        return rows((yy * 2 + e) * 64, 64)

    for er in (0, 1):
        e = (1 - zh) if er == 0 else zh
        for d in (2, 1, 3):
            s = er * 3 + d - 1
            go("ly", s, lg.at[block(ring(y, d), e)], lr.at[s], dev(y=ring(y, d)))
    for d in (1, 3, 2):
        got("ly", d - 1, lr.at[d - 1])
    lzs[...] = lg[block(y, 1 - zh), :] + lr[0] + lr[1] + lr[2]
    go("lz", 0, lzs, lzr, dev(zh=1 - zh))
    for d in (1, 3, 2):
        got("ps", d - 1, px.at[ring(x, -d)])
    pt[...] = jnp.broadcast_to(px[y].astype(F32)[0:1], (128, 128)).T
    for d in (1, 3, 2):
        got("ly", 3 + d - 1, lr.at[3 + d - 1])
    eb[...] = lg[block(y, zh), :] + lr[3] + lr[4] + lr[5]
    got("lz", 0, lzr)
    logits = LOGIT_SCALE * (eb[...] + lzr[...])

    cols = lax.broadcasted_iota(jnp.int32, (64, 1024), 1)
    answer = (cols // 256) * 1024 + x * 256 + cols % 256
    positive = pt[rows(zh * 64, 64), 0:1].astype(jnp.int32)
    hit = answer == positive
    ex = jnp.exp(logits)
    eb[...] = ex
    sums = jnp.concatenate(
        [
            jnp.sum(ex, axis=1, keepdims=True),
            jnp.sum(jnp.where(hit, logits, 0.0), axis=1, keepdims=True),
        ],
        axis=0,
    )
    txb[0] = to_row(sums)
    for d in (2, 1, 3):
        go("tx", d - 1, txb.at[0], txb.at[d], dev(x=ring(x, d)))
    for d in (1, 3, 2):
        got("tx", d - 1, txb.at[d])
    totals = txb[0] + txb[1] + txb[2] + txb[3]
    col = to_col(totals[0:1])
    scale = LOGIT_SCALE / col[0:64]
    score = eb[...] * scale - jnp.where(hit, LOGIT_SCALE, 0.0)
    mine = block(y, zh)
    sa[mine, :] = score.astype(BF16)

    go("sz", 0, sa.at[mine], sa.at[mine], dev(zh=1 - zh))
    for d in (2, 1, 3):
        go("sy", d - 1, sa.at[mine], sa.at[mine], dev(y=ring(y, d)))
    losses = jnp.log(totals) - jnp.concatenate([totals[:, 64:], totals[:, :64]], axis=1)
    lossb[j] = losses
    for d, e in others:
        go("pl", d * 2 + e - 1, lossb.at[j], lossb.at[j], dev(y=ring(y, d), zh=(zh + e) % 2))
    pair = block(y, 1 - zh)
    got("sz", 0, sa.at[pair])
    for d in (2, 1, 3):
        go("sy", 3 + d - 1, sa.at[pair], sa.at[pair], dev(y=ring(y, d)))
    for k in (0, 1):
        e = zh if k == 0 else 1 - zh
        for d in (1, 3, 2):
            got("sy", k * 3 + d - 1, sa.at[block(ring(y, -d), e)])

    def answers_part(t):
        zz = ring(zl, t)
        gap[t] = tn(sa[:, rows(zz * 256, 256)], qx[...])
        away = rows((1 - core) * 128, 128)
        go("gc", t, gap.at[t, away], gcr.at[t], dev(core=1 - core))

    def answers_sum(t):
        got("gc", t, gcr.at[t])
        gzs[t] = gap[t, rows(core * 128, 128), :] + gcr[t]
        if t:
            go("gz", t - 1, gzs.at[t], gzr.at[t - 1], dev(zl=ring(zl, t)))

    def queries_part(d):
        gqs[d] = nn(sa[rows(ring(x, d) * 128, 128), :], aa[...])
        if d:
            go("gq", d - 1, gqs.at[d], gqr.at[d - 1], dev(x=ring(x, d)))

    answers_part(2)
    answers_part(1)
    answers_sum(2)
    answers_part(3)
    answers_sum(1)
    queries_part(2)
    answers_sum(3)
    queries_part(1)
    queries_part(3)
    answers_part(0)
    queries_part(0)
    answers_sum(0)

    def radial(h, g):
        at = pl.ds(h * 128, 128)
        ge[at, :] = g
        rb[h, 0] = to_row(jnp.sum(g * sc[at, :], axis=1, keepdims=True))
        for d, e in others:
            k = d * 2 + e
            go("rq" if h == 0 else "ra", k - 1, rb.at[h, 0], rb.at[h, k],
               dev(y=ring(y, d), zh=(zh + e) % 2))

    def spread(h):
        at = pl.ds(h * 128, 128)
        tot = rb[h, 0]
        for d, e in others[::-1]:
            k = d * 2 + e
            got("rq" if h == 0 else "ra", k - 1, rb.at[h, k])
        for k in range(1, 8):
            tot = tot + rb[h, k]
        rad = to_col(tot[0:1])
        iv = inv_s[at, 0:1]
        out = gain_ref[...] * (iv * ge[at, :] - (iv * iv * iv * rad) * sc[at, :])
        rg_ref[at, :] = out
        gg[j, at, :] = out.astype(BF16)
        go("gh", h, gg.at[j, at], gg.at[j, at], dev(zh=1 - zh))
        for d in (2, 1, 3):
            go("gy", h * 6 + d - 1, gg.at[j, at], gg.at[j, at], dev(y=ring(y, d)))

    def forward(h):
        at = pl.ds(h * 128, 128)
        jj = y * 2 + 1 - zh
        got("gh", h, gg.at[jj, at])
        for d in (2, 1, 3):
            go("gy", h * 6 + 3 + d - 1, gg.at[jj, at], gg.at[jj, at], dev(y=ring(y, d)))

    def columns(h, t):
        at = pl.ds(h * 128, 128)
        yy = ring(y, -t)
        if t:
            for k in (0, 1):
                e = zh if k == 0 else 1 - zh
                got("gy", h * 6 + k * 3 + t - 1, gg.at[yy * 2 + e, at])
        to = rows(x * 256 + h * 128, 128)
        for d in (2, 1, 3):
            xx = ring(x, d)
            src = gg.at[yy * 2 + xx // 2, at, rows((xx % 2) * 256, 256)]
            go("gx", (t * 2 + h) * 3 + d - 1, src, gx.at[t, to], dev(x=xx))
        gx[t, to, :] = gg[yy * 2 + x // 2, at, rows((x % 2) * 256, 256)]

    for d in (1, 3, 2):
        got("gq", d - 1, gqr.at[d - 1])
    radial(0, gqs[0] + gqr[0] + gqr[1] + gqr[2])
    spread(0)
    for d in (1, 3, 2):
        got("gz", d - 1, gzr.at[d - 1])
    radial(1, gzs[0] + gzr[0] + gzr[1] + gzr[2])
    forward(0)
    spread(1)
    columns(0, 0)
    columns(0, 1)
    forward(1)
    columns(1, 0)
    columns(0, 3)
    columns(0, 2)

    for d in (1, 3, 2):
        got("ax", d - 1, ax.at[rows(ring(x, -d) * 256, 256)])

    def weight_part(t):
        for h in (0, 1):
            for d in (1, 3, 2):
                got("gx", (t * 2 + h) * 3 + d - 1,
                    gx.at[t, rows(ring(x, -d) * 256 + h * 128, 128)])
        part = tn(ax[...], gx[t])
        tb[t, 0] = part[:, 0:128]
        tb[t, 1] = part[:, 128:256]
        go("wc", t, tb.at[t, 1 - core], tcr.at[t], dev(core=1 - core))

    def weight_sum(t):
        got("wc", t, tcr.at[t])
        zz = ring(y, -t)
        d = (zz - zl + 4) % 4
        wzs[d] = tb[t, core] + tcr[t]

        @pl.when(d > 0)
        def _():
            copy("wz", d - 1, wzs.at[d], wzr.at[d - 1], dev(zl=zz)).start()

    weight_part(0)
    columns(1, 1)
    weight_sum(0)
    weight_part(1)
    columns(1, 3)
    weight_sum(1)
    weight_part(3)
    columns(1, 2)
    weight_sum(3)
    weight_part(2)
    weight_sum(2)

    def attn_part(jj, acc):
        return acc + nt(gg[jj], w_ref[:, rows(jj * 512, 512)])

    ag_ref[...] = lax.fori_loop(0, 8, attn_part, jnp.zeros((256, 512), F32))

    for d, e in others:
        jj = ring(y, -d) * 2 + (zh + e) % 2
        got("pl", d * 2 + e - 1, lossb.at[jj])
    loss_ref[...] = jnp.concatenate(
        [lossb[x * 2][0:1, 0:64], lossb[x * 2 + 1][0:1, 0:64]], axis=1
    )
    for d in (1, 3, 2):
        got("wz", d - 1, wzr.at[d - 1])
    wg_ref[...] = wzs[0] + wzr[0] + wzr[1] + wzr[2]
    for c in pending:
        c.wait_send()
    for d in (1, 2, 3):
        copy("wz", d - 1, wzs.at[d], wzr.at[d - 1], dev(core=1 - core)).wait_send()


def body(attn_out, residual, o_weight, norm_gain, positive):
    vmem = pl.BlockSpec(memory_space=pltpu.VMEM)
    shape = jax.ShapeDtypeStruct
    scratch = [
        ((6, 256, 512), WIRE), ((6, 256, 512), WIRE), ((2, 256, 512), F32),
        ((256, 512), WIRE), ((256, 512), WIRE), ((256, 512), F32), ((256, 128), F32),
        ((8, 8, 256), F32),
        ((512, 512), BF16), ((1024, 512), BF16), ((4, 8, 128), jnp.int32), ((128, 128), F32),
        ((512, 1024), F32), ((6, 64, 1024), F32), ((64, 1024), F32), ((64, 1024), F32),
        ((64, 1024), F32), ((4, 8, 128), F32), ((8, 8, 128), F32),
        ((512, 1024), BF16), ((4, 256, 512), F32), ((4, 128, 512), F32), ((4, 128, 512), F32),
        ((3, 128, 512), F32), ((4, 128, 512), F32), ((3, 128, 512), F32), ((256, 512), F32),
        ((2, 8, 8, 128), F32),
        ((8, 256, 512), BF16), ((4, 1024, 256), BF16), ((1024, 512), BF16),
        ((4, 2, 512, 128), F32), ((4, 512, 128), F32), ((4, 512, 128), F32),
        ((3, 512, 128), F32),
    ]
    loss, rg, ag, wg = pl.pallas_call(
        kernel,
        name="step",
        out_shape=(
            shape((1, 128), F32), shape((256, 512), F32), shape((256, 512), F32),
            shape((512, 128), F32),
        ),
        in_specs=[vmem] * 5,
        out_specs=[vmem] * 4,
        scratch_shapes=[pltpu.VMEM(s, t) for s, t in scratch]
        + [pltpu.SemaphoreType.DMA((COUNT,)), pltpu.SemaphoreType.DMA((COUNT,))],
        compiler_params=pltpu.CompilerParams(
            collective_id=0, has_side_effects=True, vmem_limit_bytes=56 * 1024 * 1024
        ),
    )(
        attn_out.reshape(256, 512), residual.reshape(256, 512), o_weight,
        norm_gain.reshape(1, 512), positive.reshape(1, 128),
    )
    return (
        loss.reshape(128), rg.reshape(2, 128, 512), ag.reshape(2, 128, 512), wg,
    )


def solution(mesh):
    placed = (P(None, "dp", "mp"), P(None, "dp", "mp"), P("mp", None), P("mp"), P("dp"))
    return jax.shard_map(
        body,
        mesh=mesh,
        in_specs=placed,
        out_specs=(P("dp"), P(None, "dp", "mp"), P(None, "dp", "mp"), P("mp", "dp")),
        check_vma=False,
    )
```

time: 864 us -> 204 us (0.24)
  the two profiles are of different devices: /device:TPU:8 before, /device:TPU:63 now
where the time goes in v1:
time: 204 us; the launch traced here: 203 us
  Pallas kernels  196 us (96%)
  local copies, waits for them, and re-layouts  6.52 us (3%)
    pallas_call x1, Pallas kernels, body(): pl.pallas_call(kernel, name='step', out_shape=(shape((1, 128), F32), shap...  196 us
    unnamed x4, local copies, waits for them, and re-layouts  6.52 us

profile of v1, /device:TPU:63, one launch (start us, length us, event | category | flops | bytes accessed | tf_op | source)
XLA Modules:
  0.0 203.1 jit_solution(9187899309782226446)
XLA Ops:
  0.6 195.9 %step.1 = (f32[1,128]{1,0:T(1,128)}, f32[256,512]{1,0:T(8,128)}, f32[256,512]{1,0:T(8,128)}, f32[512,128]{1,0:T(8,128)}) custom-call(bf16[256,512]{1,0:T(8,128)(2,1)} %bitcast.9, bf16[256,512]{1,0:T(8,128)(2,1)} %bitcast.10, bf16[512,4096]{1,0:T(8,128)(2,1)} %w_ref.1, f32[1,512]{1,0:T(1,128)} %bitcast.11, s32[1,128]{1,0:T(1,128)} %bitcast.12), custom_call_target="tpu_custom_call" | custom-call | tf_op jit(solution)/shard_map/step/pallas_call | solution.py:393
  196.6 1.1 copy.13
  197.7 1.9 copy.14
  199.6 1.9 copy.15
  201.4 1.7 copy.16

commit v2 on v1

v2 whole, which is shorter than its diff:
```python
import jax
import jax.numpy as jnp
from jax import lax
from jax.sharding import PartitionSpec as P
from jax.experimental import pallas as pl
from jax.experimental.pallas import tpu as pltpu

LOGIT_SCALE = 50.0
EPS = 1e-06
F32 = jnp.float32
BF16 = jnp.bfloat16
MESH = pl.DeviceIdType.MESH
WIRE = BF16
GZ_WIRE = F32
WZ_WIRE = F32

STAGES = dict(
    y1=12, z1=2, ss=14, qx=3, ps=3, ax=3, az=3, ac=4, ly=24, lz=4, tx=3, td=7,
    ez=4, ey=24, gc=4, gz=3, gq=3, rr=14, gh=4, gy=24, gx=24, wc=4, wz=3,
)
BASE = {}
COUNT = 0
for _name, _n in STAGES.items():
    BASE[_name] = COUNT
    COUNT += _n


def nt(a, b):
    return lax.dot_general(a, b, (((1,), (1,)), ((), ())), preferred_element_type=F32)


def tn(a, b):
    return lax.dot_general(a, b, (((0,), (0,)), ((), ())), preferred_element_type=F32)


def nn(a, b):
    return lax.dot_general(a, b, (((1,), (0,)), ((), ())), preferred_element_type=F32)


def to_row(col):
    n = col.shape[0]
    return jnp.broadcast_to(col, (n, 128)).T[0:8]


def to_col(row):
    n = row.shape[1]
    return jnp.broadcast_to(row, (128, n)).T[:, 0:1]


def rows(start, size, unit=None):
    return pl.ds(pl.multiple_of(start, unit or size), size)


def kernel(
    a_ref, r_ref, w_ref, gain_ref, pos_ref,
    loss_ref, rg_ref, ag_ref, wg_ref,
    ys, yr, own, zs, zr, sc, inv_s, ssb,
    qx, aa, px, pc, lg, lr, lzs, lzr, pos_s, sums_s, txb, td,
    ea, sa, gap, gcr, gzs, gzr, gqs, gqr, ge, rb,
    gg, gx, ax, tb, tcr, wzs, wzr,
    send, recv,
):
    dp = lax.axis_index("dp")
    mp = lax.axis_index("mp")
    core, x, zl = dp % 2, (dp // 2) % 4, dp // 8
    y, zh = mp // 2, mp % 2
    j = mp
    pending = []

    def dev(core=core, x=x, zl=zl, y=y, zh=zh):
        return ((zl * 4 + x) * 2 + core, y * 2 + zh)

    def copy(stage, k, src, dst, to):
        return pltpu.make_async_remote_copy(
            src_ref=src, dst_ref=dst,
            send_sem=send.at[BASE[stage] + k], recv_sem=recv.at[BASE[stage] + k],
            device_id=to, device_id_type=MESH,
        )

    def go(*args):
        c = copy(*args)
        c.start()
        pending.append(c)

    def got(stage, k, dst):
        copy(stage, k, dst, dst, dev(core=1 - core)).wait_recv()

    def ring(v, d):
        return (v + d) % 4

    others = [(d, e) for d in (2, 1, 3, 0) for e in (1, 0) if (d, e) != (0, 0)]

    barrier = pltpu.get_barrier_semaphore()
    peers = [dev(y=ring(y, d), zh=(zh + e) % 2) for d, e in others]
    peers += [dev(x=ring(x, d)) for d in (1, 2, 3)]
    peers += [dev(zl=ring(zl, d)) for d in (1, 2, 3)]
    peers += [dev(core=1 - core)]
    for p in peers:
        pl.semaphore_signal(barrier, inc=1, device_id=p, device_id_type=MESH)

    def half(h):
        return pl.ds(h * 128, 128)

    def product(h, yy, er):
        e = (1 - zh) if er == 0 else zh
        return nn(a_ref[half(h), :], w_ref[:, rows(yy * 1024 + e * 512, 512)])

    def y_products(h):
        for er in (0, 1):
            for d in (2, 1, 3):
                ys[h * 2 + er, d - 1] = product(h, ring(y, d), er).astype(WIRE)

    def y_send(h):
        for er in (0, 1):
            c = h * 2 + er
            for d in (2, 1, 3):
                go("y1", c * 3 + d - 1, ys.at[c, d - 1], yr.at[c, d - 1], dev(y=ring(y, d)))

    def y_sum(c):
        for d in (1, 3, 2):
            got("y1", c * 3 + d - 1, yr.at[c, d - 1])
        return own[c] + yr[c, 0].astype(F32) + yr[c, 1].astype(F32) + yr[c, 2].astype(F32)

    def z_send(h):
        zs[h] = y_sum(h * 2).astype(WIRE)
        go("z1", h, zs.at[h], zr.at[h], dev(zh=1 - zh))

    def squares(h):
        got("z1", h, zr.at[h])
        proj = own[h * 2 + 1] + zr[h].astype(F32)
        scaled = (r_ref[half(h), :].astype(F32) + proj) * gain_ref[...]
        sc[half(h), :] = scaled
        ssb[h, 0] = to_row(jnp.sum(scaled * scaled, axis=1, keepdims=True))
        for d, e in others:
            k = d * 2 + e
            go("ss", h * 7 + k - 1, ssb.at[h, 0], ssb.at[h, k], dev(y=ring(y, d), zh=(zh + e) % 2))

    def embed(h):
        for d, e in others[::-1]:
            k = d * 2 + e
            got("ss", h * 7 + k - 1, ssb.at[h, k])
        total = ssb[h, 0]
        for k in range(1, 8):
            total = total + ssb[h, k]
        inv = to_col(lax.rsqrt(total[0:1] + EPS))
        inv_s[half(h), :] = jnp.broadcast_to(inv, (128, 128))
        return (sc[half(h), :] * inv).astype(BF16)

    y_products(0)
    px[x] = jnp.broadcast_to(pos_ref[...], (8, 128))
    pl.semaphore_wait(barrier, len(peers))
    y_send(0)
    y_products(1)
    y_send(1)
    for d in (2, 1, 3):
        go("ps", d - 1, px.at[x], px.at[x], dev(x=ring(x, d)))
        go("ax", d - 1, a_ref, ax.at[rows(x * 256, 256)], dev(x=ring(x, d)))
    for h in (0, 1):
        for er in (0, 1):
            own[h * 2 + er] = product(h, y, er)
    ax[rows(x * 256, 256), :] = a_ref[...]

    z_send(0)
    own[1] = y_sum(1)
    z_send(1)
    squares(0)
    emb = embed(0)
    q_at = rows(x * 128, 128)
    qx[q_at, :] = emb
    for d in (2, 1, 3):
        go("qx", d - 1, qx.at[q_at], qx.at[q_at], dev(x=ring(x, d)))
    own[3] = y_sum(3)
    squares(1)
    for d in (1, 3, 2):
        got("ps", d - 1, px.at[ring(x, -d)])
    for xx in range(4):
        pc[pl.ds(xx * 128, 128), :] = jnp.broadcast_to(
            to_col(px[xx].astype(F32)[0:1]), (128, 128)
        )
    for d in (1, 3, 2):
        got("qx", d - 1, qx.at[rows(ring(x, -d) * 128, 128)])
    emb = embed(1)

    a_at = rows((zl * 2 + core) * 128, 128)
    aa[a_at, :] = emb
    go("ac", 0, aa.at[a_at], aa.at[a_at], dev(core=1 - core))
    for d in (2, 1, 3):
        go("az", d - 1, aa.at[a_at], aa.at[a_at], dev(zl=ring(zl, d)))

    def block(yy, e):
        return rows((yy * 2 + e) * 64, 64)

    mine, pair = block(y, zh), block(y, 1 - zh)

    def logit_send(t):
        zz = ring(zl, -t)
        if t:
            at = rows((zz * 2 + core) * 128, 128)
            got("az", t - 1, aa.at[at])
            go("ac", t, aa.at[at], aa.at[at], dev(core=1 - core))
        got("ac", t, aa.at[rows((zz * 2 + 1 - core) * 128, 128)])
        lg[t] = nt(qx[...], aa[rows(zz * 256, 256), :])
        for er in (0, 1):
            e = (1 - zh) if er == 0 else zh
            for d in (2, 1, 3):
                k = er * 3 + d - 1
                go("ly", t * 6 + k, lg.at[t, block(ring(y, d), e)], lr.at[t, k], dev(y=ring(y, d)))

    def logit_pass(t):
        for d in (1, 3, 2):
            got("ly", t * 6 + d - 1, lr.at[t, d - 1])
        lzs[t] = lg[t, pair, :] + lr[t, 0] + lr[t, 1] + lr[t, 2]
        go("lz", t, lzs.at[t], lzr.at[t], dev(zh=1 - zh))

    def hits(t, positive):
        n = positive.shape[0]
        cols = lax.broadcasted_iota(jnp.int32, (n, 256), 1).astype(F32)
        first = (ring(zl, -t) * 1024 + x * 256).astype(F32)
        return cols == positive - first

    def logit_done(t):
        for d in (1, 3, 2):
            got("ly", t * 6 + 3 + d - 1, lr.at[t, 3 + d - 1])
        got("lz", t, lzr.at[t])
        logits = LOGIT_SCALE * (lg[t, mine, :] + lr[t, 3] + lr[t, 4] + lr[t, 5] + lzr[t])
        ex = jnp.exp(logits)
        ea[t, mine, :] = ex.astype(BF16)
        go("ez", t, ea.at[t, mine], ea.at[t, mine], dev(zh=1 - zh))
        for d in (2, 1, 3):
            go("ey", t * 6 + d - 1, ea.at[t, mine], ea.at[t, mine], dev(y=ring(y, d)))
        hit = hits(t, pc[mine, 0:1])
        sums_s[t] = jnp.concatenate(
            [
                jnp.sum(ex, axis=1, keepdims=True),
                jnp.sum(jnp.where(hit, logits, 0.0), axis=1, keepdims=True),
            ],
            axis=0,
        )

    def exp_pass(t):
        got("ez", t, ea.at[t, pair])
        for d in (2, 1, 3):
            go("ey", t * 6 + 3 + d - 1, ea.at[t, pair], ea.at[t, pair], dev(y=ring(y, d)))

    logit_send(0)
    logit_send(1)
    logit_pass(0)
    logit_send(3)
    logit_send(2)
    logit_pass(1)
    logit_done(0)
    logit_pass(3)
    logit_done(1)
    exp_pass(0)
    logit_pass(2)
    logit_done(3)
    exp_pass(1)
    logit_done(2)

    txb[0] = to_row(sums_s[0] + sums_s[1] + sums_s[2] + sums_s[3])
    for d in (2, 1, 3):
        go("tx", d - 1, txb.at[0], txb.at[d], dev(x=ring(x, d)))
    exp_pass(3)
    for d in (1, 3, 2):
        got("tx", d - 1, txb.at[d])
    td[j] = txb[0] + txb[1] + txb[2] + txb[3]
    for d, e in others:
        go("td", d * 2 + e - 1, td.at[j], td.at[j], dev(y=ring(y, d), zh=(zh + e) % 2))
    exp_pass(2)

    for d, e in others[::-1]:
        got("td", d * 2 + e - 1, td.at[ring(y, -d) * 2 + (zh + e) % 2])
    for xx in range(4):
        first, second = td[xx * 2][0:1], td[xx * 2 + 1][0:1]
        total = jnp.concatenate([first[:, 0:64], second[:, 0:64]], axis=1)
        top = jnp.concatenate([first[:, 64:128], second[:, 64:128]], axis=1)
        scale = LOGIT_SCALE / total
        at = pl.ds(xx * 128, 128)
        pos_s[0, at, :] = jnp.broadcast_to(to_col(scale), (128, 128))
        pos_s[1, at, :] = jnp.broadcast_to(
            to_col(jnp.exp(top) * scale - LOGIT_SCALE), (128, 128)
        )

    def score(t):
        for k in (0, 1):
            e = zh if k == 0 else 1 - zh
            for d in (1, 3, 2):
                got("ey", t * 6 + k * 3 + d - 1, ea.at[t, block(ring(y, -d), e)])
        for xx in range(4):
            at = pl.ds(xx * 128, 128)
            rest = ea[t, at, :].astype(F32) * pos_s[0, at, 0:1]
            sa[t, at, :] = jnp.where(
                hits(t, pc[at, 0:1]), pos_s[1, at, 0:1], rest
            ).astype(BF16)

    def answers_part(t):
        gap[t] = tn(sa[t], qx[...])
        away = rows((1 - core) * 128, 128)
        go("gc", t, gap.at[t, away], gcr.at[t], dev(core=1 - core))

    def answers_sum(t):
        got("gc", t, gcr.at[t])
        both = gap[t, rows(core * 128, 128), :] + gcr[t]
        if t:
            gzs[t] = both.astype(GZ_WIRE)
            go("gz", t - 1, gzs.at[t], gzr.at[t - 1], dev(zl=ring(zl, -t)))
        else:
            ge[half(1), :] = both

    def queries_part(d):
        part = jnp.zeros((128, 512), F32)
        for t in range(4):
            left = sa[t, rows(ring(x, d) * 128, 128), :]
            part = part + nn(left, aa[rows(ring(zl, -t) * 256, 256), :])
        gqs[d] = part
        if d:
            go("gq", d - 1, gqs.at[d], gqr.at[d - 1], dev(x=ring(x, d)))

    score(2)
    answers_part(2)
    score(3)
    answers_part(3)
    answers_sum(2)
    score(1)
    answers_part(1)
    answers_sum(3)
    score(0)
    queries_part(2)
    answers_sum(1)
    queries_part(1)
    queries_part(3)
    answers_part(0)
    queries_part(0)
    answers_sum(0)

    def radial(h, g):
        at = half(h)
        ge[at, :] = g
        rb[h, 0] = to_row(jnp.sum(g * sc[at, :], axis=1, keepdims=True))
        for d, e in others:
            k = d * 2 + e
            go("rr", h * 7 + k - 1, rb.at[h, 0], rb.at[h, k], dev(y=ring(y, d), zh=(zh + e) % 2))

    def spread(h):
        at = half(h)
        tot = rb[h, 0]
        for d, e in others[::-1]:
            k = d * 2 + e
            got("rr", h * 7 + k - 1, rb.at[h, k])
        for k in range(1, 8):
            tot = tot + rb[h, k]
        rad = to_col(tot[0:1])
        iv = inv_s[at, 0:1]
        out = gain_ref[...] * (iv * ge[at, :] - (iv * iv * iv * rad) * sc[at, :])
        rg_ref[at, :] = out
        for c in (0, 1):
            gg[j, c, at, :] = out[:, c * 256:(c + 1) * 256].astype(BF16)
        for c in (0, 1):
            part = gg.at[j, c, at]
            go("gh", h * 2 + c, part, part, dev(zh=1 - zh))
        for c in (0, 1):
            part = gg.at[j, c, at]
            for d in (2, 1, 3):
                go("gy", h * 12 + c * 3 + d - 1, part, part, dev(y=ring(y, d)))

    def forward(h):
        for c in (0, 1):
            part = gg.at[y * 2 + 1 - zh, c, half(h)]
            got("gh", h * 2 + c, part)
            for d in (2, 1, 3):
                go("gy", h * 12 + 6 + c * 3 + d - 1, part, part, dev(y=ring(y, d)))

    def columns(h, t):
        at = half(h)
        yy = ring(y, -t)
        if t:
            for k in (0, 1):
                e = zh if k == 0 else 1 - zh
                for c in (0, 1):
                    got("gy", h * 12 + k * 6 + c * 3 + t - 1, gg.at[yy * 2 + e, c, at])
        to = rows(x * 256 + h * 128, 128)
        for d in (2, 1, 3):
            xx = ring(x, d)
            src = gg.at[yy * 2 + xx // 2, xx % 2, at]
            go("gx", (t * 2 + h) * 3 + d - 1, src, gx.at[t, to], dev(x=xx))
        gx[t, to, :] = gg[yy * 2 + x // 2, x % 2, at, :]

    for d in (1, 3, 2):
        got("gq", d - 1, gqr.at[d - 1])
    radial(0, gqs[0] + gqr[0] + gqr[1] + gqr[2])
    spread(0)
    for d in (1, 3, 2):
        got("gz", d - 1, gzr.at[d - 1])
    radial(1, ge[half(1), :] + gzr[0].astype(F32) + gzr[1].astype(F32) + gzr[2].astype(F32))
    forward(0)
    spread(1)
    columns(0, 0)
    columns(0, 1)
    forward(1)
    columns(1, 0)
    columns(0, 3)
    columns(0, 2)

    for d in (1, 3, 2):
        got("ax", d - 1, ax.at[rows(ring(x, -d) * 256, 256)])

    def weight_part(t):
        for h in (0, 1):
            for d in (1, 3, 2):
                got("gx", (t * 2 + h) * 3 + d - 1,
                    gx.at[t, rows(ring(x, -d) * 256 + h * 128, 128)])
        part = tn(ax[...], gx[t])
        tb[t, 0] = part[:, 0:128]
        tb[t, 1] = part[:, 128:256]
        go("wc", t, tb.at[t, 1 - core], tcr.at[t], dev(core=1 - core))

    def weight_sum(t):
        got("wc", t, tcr.at[t])
        zz = ring(y, -t)
        d = (zz - zl + 4) % 4
        both = tb[t, core] + tcr[t]

        @pl.when(d > 0)
        def _():
            wzs[d - 1] = both.astype(WZ_WIRE)
            copy("wz", d - 1, wzs.at[d - 1], wzr.at[d - 1], dev(zl=zz)).start()

        @pl.when(d == 0)
        def _():
            wg_ref[...] = both

    weight_part(0)
    columns(1, 1)
    weight_sum(0)
    weight_part(1)
    columns(1, 3)
    weight_sum(1)
    columns(1, 2)
    weight_part(3)
    weight_sum(3)

    ag_ref[...] = jnp.zeros((256, 512), F32)
    for jj in range(8):
        for c in (0, 1):
            ag_ref[...] += nt(gg[jj, c], w_ref[:, pl.ds(jj * 512 + c * 256, 256)])
    weight_part(2)
    weight_sum(2)
    losses = [
        jnp.log(v[:, 0:64]) - v[:, 64:128] for v in (td[x * 2][0:1], td[x * 2 + 1][0:1])
    ]
    loss_ref[...] = jnp.concatenate(losses, axis=1)
    for d in (1, 3, 2):
        got("wz", d - 1, wzr.at[d - 1])
    wg_ref[...] += wzr[0].astype(F32) + wzr[1].astype(F32) + wzr[2].astype(F32)
    for c in pending:
        c.wait_send()
    for d in (1, 2, 3):
        copy("wz", d - 1, wzs.at[d - 1], wzr.at[d - 1], dev(core=1 - core)).wait_send()


def hand_over(*refs):
    for k in range(4):
        refs[4 + k][...] = refs[k][...]


def body(attn_out, residual, o_weight, norm_gain, positive):
    vmem = pl.BlockSpec(memory_space=pltpu.VMEM)
    shape = jax.ShapeDtypeStruct
    scratch = [
        ((4, 3, 128, 512), WIRE), ((4, 3, 128, 512), WIRE), ((4, 128, 512), F32),
        ((2, 128, 512), WIRE), ((2, 128, 512), WIRE), ((256, 512), F32), ((256, 128), F32),
        ((2, 8, 8, 128), F32),
        ((512, 512), BF16), ((1024, 512), BF16), ((4, 8, 128), jnp.int32), ((512, 128), F32),
        ((4, 512, 256), F32), ((4, 6, 64, 256), F32), ((4, 64, 256), F32), ((4, 64, 256), F32),
        ((2, 512, 128), F32), ((4, 128, 1), F32), ((4, 8, 128), F32), ((8, 8, 128), F32),
        ((4, 512, 256), BF16), ((4, 512, 256), BF16),
        ((4, 256, 512), F32), ((4, 128, 512), F32), ((4, 128, 512), GZ_WIRE),
        ((3, 128, 512), GZ_WIRE), ((4, 128, 512), F32), ((3, 128, 512), F32), ((256, 512), F32),
        ((2, 8, 8, 128), F32),
        ((8, 2, 256, 256), BF16), ((4, 1024, 256), BF16), ((1024, 512), BF16),
        ((4, 2, 512, 128), F32), ((4, 512, 128), F32), ((3, 512, 128), WZ_WIRE),
        ((3, 512, 128), WZ_WIRE),
    ]
    outs = (
        shape((1, 128), F32), shape((256, 512), F32), shape((256, 512), F32),
        shape((512, 128), F32),
    )
    made = pl.pallas_call(
        kernel,
        name="step",
        out_shape=outs,
        in_specs=[vmem] * 5,
        out_specs=[vmem] * 4,
        scratch_shapes=[pltpu.VMEM(s, t) for s, t in scratch]
        + [pltpu.SemaphoreType.DMA((COUNT,)), pltpu.SemaphoreType.DMA((COUNT,))],
        compiler_params=pltpu.CompilerParams(
            collective_id=0, has_side_effects=True, vmem_limit_bytes=56 * 1024 * 1024
        ),
    )(
        attn_out.reshape(256, 512), residual.reshape(256, 512), o_weight,
        norm_gain.reshape(1, 512), positive.reshape(1, 128),
    )
    loss, rg, ag, wg = pl.pallas_call(
        hand_over,
        name="hand_over",
        out_shape=outs,
        in_specs=[vmem] * 4,
        out_specs=[vmem] * 4,
    )(*made)
    return (
        loss.reshape(128), rg.reshape(2, 128, 512), ag.reshape(2, 128, 512), wg,
    )


def solution(mesh):
    placed = (P(None, "dp", "mp"), P(None, "dp", "mp"), P("mp", None), P("mp"), P("dp"))
    return jax.shard_map(
        body,
        mesh=mesh,
        in_specs=placed,
        out_specs=(P("dp"), P(None, "dp", "mp"), P(None, "dp", "mp"), P("mp", "dp")),
        check_vma=False,
    )
```

time: 204 us -> 185 us (0.907)
  Pallas kernels: 196 us -> 184 us
  local copies, waits for them, and re-layouts: 6.52 us -> 0 us
    pallas_call x1 -> x2, Pallas kernels: 196 us -> 184 us  [the longest x1 181 us: body(): pl.pallas_call(kernel, name='step', out_shape=outs, in_specs=[vmem] * 5,...]
    unnamed x4 -> x0, local copies, waits for them, and re-layouts: 6.52 us -> none
where the time goes in v2:
time: 185 us; the launch traced here: 184 us
  Pallas kernels  184 us (99%)
    pallas_call x1, Pallas kernels, body(): pl.pallas_call(kernel, name='step', out_shape=outs, in_specs=[vmem] * 5,...  181 us

profile of v2, /device:TPU:63, one launch (start us, length us, event | category | flops | bytes accessed | tf_op | source)
XLA Modules:
  0.0 184.3 jit_solution(14304018067906948627)
XLA Ops:
  0.6 181.3 %step.1 = (f32[1,128]{1,0:T(1,128)}, f32[256,512]{1,0:T(8,128)}, f32[256,512]{1,0:T(8,128)}, f32[512,128]{1,0:T(8,128)}) custom-call(bf16[256,512]{1,0:T(8,128)(2,1)} %bitcast.7, bf16[256,512]{1,0:T(8,128)(2,1)} %bitcast.8, bf16[512,4096]{1,0:T(8,128)(2,1)} %w_ref.1, f32[1,512]{1,0:T(1,128)} %bitcast.9, s32[1,128]{1,0:T(1,128)} %bitcast.10), custom_call_target="tpu_custom_call" | custom-call | tf_op jit(solution)/shard_map/step/pallas_call | solution.py:488
  181.9 2.4 %hand_over.1 = (f32[1,128]{1,0:T(1,128)}, f32[256,512]{1,0:T(8,128)}, f32[256,512]{1,0:T(8,128)}, f32[512,128]{1,0:T(8,128)}) custom-call(f32[1,128]{1,0:T(1,128)} %get-tuple-element.12.refs_0_, f32[256,512]{1,0:T(8,128)} %get-tuple-element.13.refs_1_, f32[256,512]{1,0:T(8,128)} %get-tuple-element.14.refs_2_, f32[512,128]{1,0:T(8,128)} %get-tuple-element.15.refs_3_), custom_call_target="tpu_custom_call" | custom-call | tf_op jit(solution)/shard_map/hand_over/pallas_call | solution.py:503

commit v3 on v2

--- a/solution.py
+++ b/solution.py
@@ -11,12 +11,12 @@
 BF16 = jnp.bfloat16
 MESH = pl.DeviceIdType.MESH
 WIRE = BF16
-GZ_WIRE = F32
-WZ_WIRE = F32
+GZ_WIRE = BF16
+WZ_WIRE = BF16
 
 STAGES = dict(
-    y1=12, z1=2, ss=14, qx=3, ps=3, ax=3, az=3, ac=4, ly=24, lz=4, tx=3, td=7,
-    ez=4, ey=24, gc=4, gz=3, gq=3, rr=14, gh=4, gy=24, gx=24, wc=4, wz=3,
+    y1=24, z1=2, ss=14, qx=3, ps=3, ax=3, az=3, ac=4, ly=48, lz=4, tx=3, td=7,
+    ez=4, ey=24, gc=4, gz=3, gq=3, rr=14, gh=4, gy=24, gx=32, wc=4, wz=3,
 )
 BASE = {}
 COUNT = 0
@@ -54,8 +54,8 @@
 def kernel(
     a_ref, r_ref, w_ref, gain_ref, pos_ref,
     loss_ref, rg_ref, ag_ref, wg_ref,
-    ys, yr, own, zs, zr, sc, inv_s, ssb,
-    qx, aa, px, pc, lg, lr, lzs, lzr, pos_s, sums_s, txb, td,
+    ys, yf, yt, yr, own, zs, zr, sc, inv_s, ssb,
+    qx, aa, px, pc, lg, lt, lr, lzs, lzr, pos_s, sums_s, txb, td,
     ea, sa, gap, gcr, gzs, gzr, gqs, gqr, ge, rb,
     gg, gx, ax, tb, tcr, wzs, wzr,
     send, recv,
@@ -70,10 +70,11 @@
     def dev(core=core, x=x, zl=zl, y=y, zh=zh):
         return ((zl * 4 + x) * 2 + core, y * 2 + zh)
 
-    def copy(stage, k, src, dst, to):
+    def copy(stage, k, src, dst, to, r=None):
         return pltpu.make_async_remote_copy(
             src_ref=src, dst_ref=dst,
-            send_sem=send.at[BASE[stage] + k], recv_sem=recv.at[BASE[stage] + k],
+            send_sem=send.at[BASE[stage] + k],
+            recv_sem=recv.at[BASE[stage] + (k if r is None else r)],
             device_id=to, device_id_type=MESH,
         )
 
@@ -105,21 +106,40 @@
         e = (1 - zh) if er == 0 else zh
         return nn(a_ref[half(h), :], w_ref[:, rows(yy * 1024 + e * 512, 512)])
 
+    low, high = pl.ds(0, 64), pl.ds(64, 64)
+    right, left = dev(y=ring(y, 1)), dev(y=ring(y, 3))
+
     def y_products(h):
         for er in (0, 1):
-            for d in (2, 1, 3):
-                ys[h * 2 + er, d - 1] = product(h, ring(y, d), er).astype(WIRE)
-
-    def y_send(h):
-        for er in (0, 1):
             c = h * 2 + er
-            for d in (2, 1, 3):
-                go("y1", c * 3 + d - 1, ys.at[c, d - 1], yr.at[c, d - 1], dev(y=ring(y, d)))
+            ys[c, 0] = product(h, ring(y, 2), er).astype(WIRE)
+            near = product(h, ring(y, 1), er)
+            yf[c, 0] = near[0:64]
+            ys[c, 1, high, :] = near[64:128].astype(WIRE)
+            near = product(h, ring(y, 3), er)
+            yf[c, 1] = near[64:128]
+            ys[c, 1, low, :] = near[0:64].astype(WIRE)
+
+    def y_send(c):
+        go("y1", c * 6 + 0, ys.at[c, 0, low], yt.at[c, 0], right)
+        go("y1", c * 6 + 1, ys.at[c, 0, high], yt.at[c, 1], left)
+        go("y1", c * 6 + 2, ys.at[c, 1, high], yr.at[c, 0, high], right)
+        go("y1", c * 6 + 3, ys.at[c, 1, low], yr.at[c, 1, low], left)
+
+    def y_hop(c):
+        got("y1", c * 6 + 0, yt.at[c, 0])
+        ys[c, 2, low, :] = (yf[c, 0] + yt[c, 0].astype(F32)).astype(WIRE)
+        go("y1", c * 6 + 4, ys.at[c, 2, low], yr.at[c, 0, low], right)
+        got("y1", c * 6 + 1, yt.at[c, 1])
+        ys[c, 2, high, :] = (yf[c, 1] + yt[c, 1].astype(F32)).astype(WIRE)
+        go("y1", c * 6 + 5, ys.at[c, 2, high], yr.at[c, 1, high], left)
 
     def y_sum(c):
-        for d in (1, 3, 2):
-            got("y1", c * 3 + d - 1, yr.at[c, d - 1])
-        return own[c] + yr[c, 0].astype(F32) + yr[c, 1].astype(F32) + yr[c, 2].astype(F32)
+        got("y1", c * 6 + 2, yr.at[c, 0, high])
+        got("y1", c * 6 + 3, yr.at[c, 1, low])
+        got("y1", c * 6 + 4, yr.at[c, 0, low])
+        got("y1", c * 6 + 5, yr.at[c, 1, high])
+        return own[c] + yr[c, 0].astype(F32) + yr[c, 1].astype(F32)
 
     def z_send(h):
         zs[h] = y_sum(h * 2).astype(WIRE)
@@ -147,30 +167,42 @@
         return (sc[half(h), :] * inv).astype(BF16)
 
     y_products(0)
+    y_products(1)
     px[x] = jnp.broadcast_to(pos_ref[...], (8, 128))
     pl.semaphore_wait(barrier, len(peers))
     y_send(0)
-    y_products(1)
-    y_send(1)
+    y_send(2)
     for d in (2, 1, 3):
         go("ps", d - 1, px.at[x], px.at[x], dev(x=ring(x, d)))
         go("ax", d - 1, a_ref, ax.at[rows(x * 256, 256)], dev(x=ring(x, d)))
     for h in (0, 1):
         for er in (0, 1):
             own[h * 2 + er] = product(h, y, er)
+    y_hop(0)
+    y_send(1)
+    y_hop(2)
+    y_send(3)
     ax[rows(x * 256, 256), :] = a_ref[...]
 
     z_send(0)
+    y_hop(1)
+    z_send(1)
+    y_hop(3)
     own[1] = y_sum(1)
-    z_send(1)
     squares(0)
+    own[3] = y_sum(3)
+    squares(1)
     emb = embed(0)
     q_at = rows(x * 128, 128)
     qx[q_at, :] = emb
     for d in (2, 1, 3):
         go("qx", d - 1, qx.at[q_at], qx.at[q_at], dev(x=ring(x, d)))
-    own[3] = y_sum(3)
-    squares(1)
+    emb = embed(1)
+    a_at = rows((zl * 2 + core) * 128, 128)
+    aa[a_at, :] = emb
+    go("ac", 0, aa.at[a_at], aa.at[a_at], dev(core=1 - core))
+    for d in (2, 1, 3):
+        go("az", d - 1, aa.at[a_at], aa.at[a_at], dev(zl=ring(zl, d)))
     for d in (1, 3, 2):
         got("ps", d - 1, px.at[ring(x, -d)])
     for xx in range(4):
@@ -179,13 +211,6 @@
         )
     for d in (1, 3, 2):
         got("qx", d - 1, qx.at[rows(ring(x, -d) * 128, 128)])
-    emb = embed(1)
-
-    a_at = rows((zl * 2 + core) * 128, 128)
-    aa[a_at, :] = emb
-    go("ac", 0, aa.at[a_at], aa.at[a_at], dev(core=1 - core))
-    for d in (2, 1, 3):
-        go("az", d - 1, aa.at[a_at], aa.at[a_at], dev(zl=ring(zl, d)))
 
     def block(yy, e):
         return rows((yy * 2 + e) * 64, 64)
@@ -201,34 +226,57 @@
         got("ac", t, aa.at[rows((zz * 2 + 1 - core) * 128, 128)])
         lg[t] = nt(qx[...], aa[rows(zz * 256, 256), :])
         for er in (0, 1):
-            e = (1 - zh) if er == 0 else zh
-            for d in (2, 1, 3):
-                k = er * 3 + d - 1
-                go("ly", t * 6 + k, lg.at[t, block(ring(y, d), e)], lr.at[t, k], dev(y=ring(y, d)))
+            k = t * 12 + er * 6
+            far, after, before = (logit_piece(t, er, d) for d in (2, 1, 3))
+            go("ly", k + 0, far.at[top], lt.at[t, er, 0], right)
+            go("ly", k + 1, far.at[end], lt.at[t, er, 1], left)
+            go("ly", k + 2, after.at[end], lr.at[t, er, 0, end], right)
+            go("ly", k + 3, before.at[top], lr.at[t, er, 1, top], left)
+
+    top, end = pl.ds(0, 32), pl.ds(32, 32)
+
+    def logit_piece(t, er, d):
+        return lg.at[t, block(ring(y, d), (1 - zh) if er == 0 else zh)]
+
+    def logit_hop(t):
+        for er in (0, 1):
+            k = t * 12 + er * 6
+            after, before = (logit_piece(t, er, d) for d in (1, 3))
+            got("ly", k + 0, lt.at[t, er, 0])
+            after[top, :] = after[top, :] + lt[t, er, 0]
+            go("ly", k + 4, after.at[top], lr.at[t, er, 0, top], right)
+            got("ly", k + 1, lt.at[t, er, 1])
+            before[end, :] = before[end, :] + lt[t, er, 1]
+            go("ly", k + 5, before.at[end], lr.at[t, er, 1, end], left)
+
+    def logit_sum(t, er):
+        k = t * 12 + er * 6
+        got("ly", k + 2, lr.at[t, er, 0, end])
+        got("ly", k + 3, lr.at[t, er, 1, top])
+        got("ly", k + 4, lr.at[t, er, 0, top])
+        got("ly", k + 5, lr.at[t, er, 1, end])
+        return lg[t, pair if er == 0 else mine, :] + lr[t, er, 0] + lr[t, er, 1]
 
     def logit_pass(t):
-        for d in (1, 3, 2):
-            got("ly", t * 6 + d - 1, lr.at[t, d - 1])
-        lzs[t] = lg[t, pair, :] + lr[t, 0] + lr[t, 1] + lr[t, 2]
+        lzs[t] = logit_sum(t, 0)
         go("lz", t, lzs.at[t], lzr.at[t], dev(zh=1 - zh))
 
-    def hits(t, positive):
-        n = positive.shape[0]
-        cols = lax.broadcasted_iota(jnp.int32, (n, 256), 1).astype(F32)
-        first = (ring(zl, -t) * 1024 + x * 256).astype(F32)
-        return cols == positive - first
+    lanes = lax.broadcasted_iota(jnp.int32, (128, 128), 1).astype(F32)
+
+    def hits(t, at, c):
+        first = (ring(zl, -t) * 1024 + x * 256 + c * 128).astype(F32)
+        mark = pc[at, :] - first
+        return lanes[0:mark.shape[0]] == mark
 
     def logit_done(t):
-        for d in (1, 3, 2):
-            got("ly", t * 6 + 3 + d - 1, lr.at[t, 3 + d - 1])
+        part = logit_sum(t, 1)
         got("lz", t, lzr.at[t])
-        logits = LOGIT_SCALE * (lg[t, mine, :] + lr[t, 3] + lr[t, 4] + lr[t, 5] + lzr[t])
+        logits = LOGIT_SCALE * (part + lzr[t])
         ex = jnp.exp(logits)
         ea[t, mine, :] = ex.astype(BF16)
         go("ez", t, ea.at[t, mine], ea.at[t, mine], dev(zh=1 - zh))
-        for d in (2, 1, 3):
-            go("ey", t * 6 + d - 1, ea.at[t, mine], ea.at[t, mine], dev(y=ring(y, d)))
-        hit = hits(t, pc[mine, 0:1])
+        exp_send(t, zh)
+        hit = jnp.concatenate([hits(t, mine, 0), hits(t, mine, 1)], axis=1)
         sums_s[t] = jnp.concatenate(
             [
                 jnp.sum(ex, axis=1, keepdims=True),
@@ -237,17 +285,26 @@
             axis=0,
         )
 
+    def exp_send(t, e):
+        part = ea.at[t, block(y, e)]
+        go("ey", t * 6 + e, part, part, right)
+        go("ey", t * 6 + 2 + e, part, part, left)
+        go("ey", t * 6 + 4 + e, part, part, dev(y=ring(y, 2)))
+
     def exp_pass(t):
         got("ez", t, ea.at[t, pair])
-        for d in (2, 1, 3):
-            go("ey", t * 6 + 3 + d - 1, ea.at[t, pair], ea.at[t, pair], dev(y=ring(y, d)))
+        exp_send(t, 1 - zh)
 
     logit_send(0)
     logit_send(1)
+    logit_hop(0)
+    logit_send(3)
+    logit_hop(1)
+    logit_send(2)
     logit_pass(0)
-    logit_send(3)
-    logit_send(2)
+    logit_hop(3)
     logit_pass(1)
+    logit_hop(2)
     logit_done(0)
     logit_pass(3)
     logit_done(1)
@@ -282,16 +339,18 @@
         )
 
     def score(t):
-        for k in (0, 1):
-            e = zh if k == 0 else 1 - zh
-            for d in (1, 3, 2):
-                got("ey", t * 6 + k * 3 + d - 1, ea.at[t, block(ring(y, -d), e)])
+        for e in (0, 1):
+            got("ey", t * 6 + e, ea.at[t, block(ring(y, 3), e)])
+            got("ey", t * 6 + 2 + e, ea.at[t, block(ring(y, 1), e)])
+            got("ey", t * 6 + 4 + e, ea.at[t, block(ring(y, 2), e)])
         for xx in range(4):
             at = pl.ds(xx * 128, 128)
-            rest = ea[t, at, :].astype(F32) * pos_s[0, at, 0:1]
-            sa[t, at, :] = jnp.where(
-                hits(t, pc[at, 0:1]), pos_s[1, at, 0:1], rest
-            ).astype(BF16)
+            for c in (0, 1):
+                part = pl.ds(c * 128, 128)
+                rest = ea[t, at, part].astype(F32) * pos_s[0, at, :]
+                sa[t, at, part] = jnp.where(
+                    hits(t, at, c), pos_s[1, at, :], rest
+                ).astype(BF16)
 
     def answers_part(t):
         gap[t] = tn(sa[t], qx[...])
@@ -358,48 +417,77 @@
         for c in (0, 1):
             part = gg.at[j, c, at]
             go("gh", h * 2 + c, part, part, dev(zh=1 - zh))
+        near(h, 0)
+
+    def near(h, k):
+        e = zh if k == 0 else 1 - zh
         for c in (0, 1):
-            part = gg.at[j, c, at]
-            for d in (2, 1, 3):
-                go("gy", h * 12 + c * 3 + d - 1, part, part, dev(y=ring(y, d)))
-
-    def forward(h):
+            part = gg.at[y * 2 + e, c, half(h)]
+            if k:
+                got("gh", h * 2 + c, part)
+            go("gy", h * 12 + k * 6 + c, part, part, right)
+            go("gy", h * 12 + k * 6 + 2 + c, part, part, left)
+
+    def hop(h, k):
+        e = zh if k == 0 else 1 - zh
+        part = gg.at[ring(y, 3) * 2 + e, 0, half(h)]
+        got("gy", h * 12 + k * 6, part)
+        go("gy", h * 12 + k * 6 + 4, part, part, right)
+        part = gg.at[ring(y, 1) * 2 + e, 1, half(h)]
+        got("gy", h * 12 + k * 6 + 3, part)
+        go("gy", h * 12 + k * 6 + 5, part, part, left)
+
+    def column_copy(h, t, k, c):
+        e = zh if k == 0 else 1 - zh
+        xx = e * 2 + c
+        d = (xx - x + 4) % 4
+        src = gg.at[ring(y, -t) * 2 + e, c, half(h)]
+        dst = gx.at[t, rows(x * 256 + h * 128, 128)]
+        n = t * 2 + h
+        return d, src, dst, copy("gx", (n * 2 + k) * 2 + c, src, dst, dev(x=xx), n * 3 + d - 1)
+
+    def columns(h, t, k):
+        for n, c in {0: (), 1: ((1, 1),), 3: ((2, 0),), 2: ((4, 0), (5, 1))}[t]:
+            e = zh if k == 0 else 1 - zh
+            got("gy", h * 12 + k * 6 + n, gg.at[ring(y, -t) * 2 + e, c, half(h)])
         for c in (0, 1):
-            part = gg.at[y * 2 + 1 - zh, c, half(h)]
-            got("gh", h * 2 + c, part)
-            for d in (2, 1, 3):
-                go("gy", h * 12 + 6 + c * 3 + d - 1, part, part, dev(y=ring(y, d)))
-
-    def columns(h, t):
-        at = half(h)
-        yy = ring(y, -t)
-        if t:
-            for k in (0, 1):
-                e = zh if k == 0 else 1 - zh
-                for c in (0, 1):
-                    got("gy", h * 12 + k * 6 + c * 3 + t - 1, gg.at[yy * 2 + e, c, at])
-        to = rows(x * 256 + h * 128, 128)
-        for d in (2, 1, 3):
-            xx = ring(x, d)
-            src = gg.at[yy * 2 + xx // 2, xx % 2, at]
-            go("gx", (t * 2 + h) * 3 + d - 1, src, gx.at[t, to], dev(x=xx))
-        gx[t, to, :] = gg[yy * 2 + x // 2, x % 2, at, :]
+            d, src, dst, remote = column_copy(h, t, k, c)
+
+            @pl.when(d > 0)
+            def _():
+                remote.start()
+
+            @pl.when(d == 0)
+            def _():
+                dst[...] = src[...]
 
     for d in (1, 3, 2):
         got("gq", d - 1, gqr.at[d - 1])
     radial(0, gqs[0] + gqr[0] + gqr[1] + gqr[2])
-    spread(0)
     for d in (1, 3, 2):
         got("gz", d - 1, gzr.at[d - 1])
     radial(1, ge[half(1), :] + gzr[0].astype(F32) + gzr[1].astype(F32) + gzr[2].astype(F32))
-    forward(0)
+    spread(0)
+    columns(0, 0, 0)
     spread(1)
-    columns(0, 0)
-    columns(0, 1)
-    forward(1)
-    columns(1, 0)
-    columns(0, 3)
-    columns(0, 2)
+    columns(1, 0, 0)
+    hop(0, 0)
+    columns(0, 1, 0)
+    columns(0, 3, 0)
+    hop(1, 0)
+    columns(1, 1, 0)
+    columns(1, 3, 0)
+    near(0, 1)
+    columns(0, 0, 1)
+    columns(0, 2, 0)
+    hop(0, 1)
+    columns(0, 1, 1)
+    columns(0, 3, 1)
+    columns(1, 2, 0)
+    near(1, 1)
+    columns(1, 0, 1)
+    columns(0, 2, 1)
+    hop(1, 1)
 
     for d in (1, 3, 2):
         got("ax", d - 1, ax.at[rows(ring(x, -d) * 256, 256)])
@@ -429,14 +517,14 @@
         def _():
             wg_ref[...] = both
 
+    columns(1, 1, 1)
+    columns(1, 3, 1)
     weight_part(0)
-    columns(1, 1)
+    columns(1, 2, 1)
     weight_sum(0)
     weight_part(1)
-    columns(1, 3)
+    weight_part(3)
     weight_sum(1)
-    columns(1, 2)
-    weight_part(3)
     weight_sum(3)
 
     ag_ref[...] = jnp.zeros((256, 512), F32)
@@ -456,6 +544,12 @@
         c.wait_send()
     for d in (1, 2, 3):
         copy("wz", d - 1, wzs.at[d - 1], wzr.at[d - 1], dev(core=1 - core)).wait_send()
+    for n in range(32):
+        d, _, _, remote = column_copy(n // 16, n // 4 % 4, n // 2 % 2, n % 2)
+
+        @pl.when(d > 0)
+        def _():
+            remote.wait_send()
 
 
 def hand_over(*refs):
@@ -467,11 +561,12 @@
     vmem = pl.BlockSpec(memory_space=pltpu.VMEM)
     shape = jax.ShapeDtypeStruct
     scratch = [
-        ((4, 3, 128, 512), WIRE), ((4, 3, 128, 512), WIRE), ((4, 128, 512), F32),
+        ((4, 3, 128, 512), WIRE), ((4, 2, 64, 512), F32), ((4, 2, 64, 512), WIRE),
+        ((4, 2, 128, 512), WIRE), ((4, 128, 512), F32),
         ((2, 128, 512), WIRE), ((2, 128, 512), WIRE), ((256, 512), F32), ((256, 128), F32),
         ((2, 8, 8, 128), F32),
         ((512, 512), BF16), ((1024, 512), BF16), ((4, 8, 128), jnp.int32), ((512, 128), F32),
-        ((4, 512, 256), F32), ((4, 6, 64, 256), F32), ((4, 64, 256), F32), ((4, 64, 256), F32),
+        ((4, 512, 256), F32), ((4, 2, 2, 32, 256), F32), ((4, 2, 2, 64, 256), F32), ((4, 64, 256), F32), ((4, 64, 256), F32),
         ((2, 512, 128), F32), ((4, 128, 1), F32), ((4, 8, 128), F32), ((8, 8, 128), F32),
         ((4, 512, 256), BF16), ((4, 512, 256), BF16),
         ((4, 256, 512), F32), ((4, 128, 512), F32), ((4, 128, 512), GZ_WIRE),
@@ -494,7 +589,7 @@
         scratch_shapes=[pltpu.VMEM(s, t) for s, t in scratch]
         + [pltpu.SemaphoreType.DMA((COUNT,)), pltpu.SemaphoreType.DMA((COUNT,))],
         compiler_params=pltpu.CompilerParams(
-            collective_id=0, has_side_effects=True, vmem_limit_bytes=56 * 1024 * 1024
+            collective_id=0, has_side_effects=True, vmem_limit_bytes=40 * 1024 * 1024
         ),
     )(
         attn_out.reshape(256, 512), residual.reshape(256, 512), o_weight,

time: 185 us -> 171 us (0.924)
  Pallas kernels: 184 us -> 161 us
  local copies, waits for them, and re-layouts: 0 us -> 8.26 us
    pallas_call x1, Pallas kernels: 181 us -> 159 us  [body(): pl.pallas_call(kernel, name='step', out_shape=outs, in_specs=[vmem] * 5,...]
    unnamed x0 -> x18, local copies, waits for them, and re-layouts: none -> 8.26 us
where the time goes in v3:
time: 171 us; the launch traced here: 170 us
  Pallas kernels  161 us (94%)
  local copies, waits for them, and re-layouts  8.26 us (5%)
    pallas_call x1, Pallas kernels, body(): pl.pallas_call(kernel, name='step', out_shape=outs, in_specs=[vmem] * 5,...  159 us
    unnamed x18, local copies, waits for them, and re-layouts  8.26 us

profile of v3, /device:TPU:63, one launch (start us, length us, event | category | flops | bytes accessed | tf_op | source)
XLA Modules:
  0.0 170.3 jit_solution(264516324664719844)
XLA Ops:
  0.6 0.0 copy-start
  0.6 2.2 %copy-done = bf16[512,4096]{1,0:T(8,128)(2,1)S(1)} copy-done((bf16[512,4096]{1,0:T(8,128)(2,1)S(1)}, bf16[512,4096]{1,0:T(8,128)(2,1)}, u32[]{:S(2)}) %copy-start) | copy-done | bytes 4194328
  2.8 0.0 copy-start.3
  2.8 0.9 copy-done.3
  3.8 0.0 copy-start.4
  3.8 0.9 copy-done.4
  4.7 0.0 copy-start.6
  4.7 0.7 copy-done.6
  5.4 0.0 copy-start.7
  5.4 0.7 copy-done.7
  6.1 159.0 %step.1 = (f32[1,128]{1,0:T(1,128)S(1)}, f32[256,512]{1,0:T(8,128)S(1)}, f32[256,512]{1,0:T(8,128)S(1)}, f32[512,128]{1,0:T(8,128)S(1)}) custom-call(bf16[256,512]{1,0:T(8,128)(2,1)S(1)} %bitcast.7, bf16[256,512]{1,0:T(8,128)(2,1)S(1)} %bitcast.8, bf16[512,4096]{1,0:T(8,128)(2,1)S(1)} %copy-done, f32[1,512]{1,0:T(1,128)S(1)} %bitcast.9, s32[1,128]{1,0:T(1,128)S(1)} %bitcast.10), custom_call_target="tpu_custom_call" | custom-call | tf_op jit(solution)/shard_map/step/pallas_call | solution.py:583
  165.1 0.0 copy-start.1
  165.1 0.8 copy-done.1
  165.9 0.0 copy-start.2
  165.9 0.8 copy-done.2
  166.7 0.0 copy-start.5
  166.7 0.7 copy-done.5
  167.4 0.0 copy-start.8
  167.4 0.6 copy-done.8
  168.0 2.4 %hand_over.1 = (f32[1,128]{1,0:T(1,128)}, f32[256,512]{1,0:T(8,128)}, f32[256,512]{1,0:T(8,128)}, f32[512,128]{1,0:T(8,128)}) custom-call(f32[1,128]{1,0:T(1,128)} %copy-done.8, f32[256,512]{1,0:T(8,128)} %copy-done.1, f32[256,512]{1,0:T(8,128)} %copy-done.2, f32[512,128]{1,0:T(8,128)} %copy-done.5), custom_call_target="tpu_custom_call" | custom-call | tf_op jit(solution)/shard_map/hand_over/pallas_call | solution.py:598
Async XLA Ops:
  0.6 2.2 %copy-start = (bf16[512,4096]{1,0:T(8,128)(2,1)S(1)}, bf16[512,4096]{1,0:T(8,128)(2,1)}, u32[]{:S(2)}) copy-start(bf16[512,4096]{1,0:T(8,128)(2,1)} %w_ref.1) | copy-start | bytes 12582916
  2.8 0.9 copy-start.3
  3.8 0.9 copy-start.4
  4.7 0.7 copy-start.6
  5.4 0.7 copy-start.7
  165.1 0.8 copy-start.1
  165.9 0.8 copy-start.2
  166.7 0.7 copy-start.5
  167.4 0.6 copy-start.8

commit v4 on v3

--- a/solution.py
+++ b/solution.py
@@ -52,13 +52,14 @@
 
 
 def kernel(
+    a_in, r_in, w_in, gain_in, pos_in,
+    loss_ref, rg_ref, ag_ref, wg_ref,
     a_ref, r_ref, w_ref, gain_ref, pos_ref,
-    loss_ref, rg_ref, ag_ref, wg_ref,
     ys, yf, yt, yr, own, zs, zr, sc, inv_s, ssb,
     qx, aa, px, pc, lg, lt, lr, lzs, lzr, pos_s, sums_s, txb, td,
     ea, sa, gap, gcr, gzs, gzr, gqs, gqr, ge, rb,
     gg, gx, ax, tb, tcr, wzs, wzr,
-    send, recv,
+    send, recv, load,
 ):
     dp = lax.axis_index("dp")
     mp = lax.axis_index("mp")
@@ -83,6 +84,14 @@
         c.start()
         pending.append(c)
 
+    def settle(upto):
+        while len(settled) < min(upto, len(pending)):
+            c = pending[len(settled)]
+            c.wait_send()
+            settled.append(c)
+
+    settled = []
+
     def got(stage, k, dst):
         copy(stage, k, dst, dst, dev(core=1 - core)).wait_recv()
 
@@ -98,6 +107,18 @@
     peers += [dev(core=1 - core)]
     for p in peers:
         pl.semaphore_signal(barrier, inc=1, device_id=p, device_id_type=MESH)
+
+    loads = [pltpu.make_async_copy(a_in, a_ref, load.at[0])]
+    for k in range(4):
+        part = pl.ds(k * 128, 128)
+        loads.append(pltpu.make_async_copy(w_in.at[part], w_ref.at[part], load.at[1 + k]))
+    loads.append(pltpu.make_async_copy(pos_in, pos_ref, load.at[5]))
+    loads.append(pltpu.make_async_copy(gain_in, gain_ref, load.at[6]))
+    loads.append(pltpu.make_async_copy(r_in, r_ref, load.at[7]))
+    for c in loads:
+        c.start()
+    for c in loads[:6]:
+        c.wait()
 
     def half(h):
         return pl.ds(h * 128, 128)
@@ -184,6 +205,8 @@
     y_send(3)
     ax[rows(x * 256, 256), :] = a_ref[...]
 
+    for c in loads[6:]:
+        c.wait()
     z_send(0)
     y_hop(1)
     z_send(1)
@@ -192,6 +215,8 @@
     squares(0)
     own[3] = y_sum(3)
     squares(1)
+    early = len(pending)
+    settle(early - 14)
     emb = embed(0)
     q_at = rows(x * 128, 128)
     qx[q_at, :] = emb
@@ -305,6 +330,7 @@
     logit_hop(3)
     logit_pass(1)
     logit_hop(2)
+    settle(early)
     logit_done(0)
     logit_pass(3)
     logit_done(1)
@@ -312,6 +338,8 @@
     logit_pass(2)
     logit_done(3)
     exp_pass(1)
+    early = len(pending) - 24
+    settle(early)
     logit_done(2)
 
     txb[0] = to_row(sums_s[0] + sums_s[1] + sums_s[2] + sums_s[3])
@@ -324,6 +352,8 @@
     for d, e in others:
         go("td", d * 2 + e - 1, td.at[j], td.at[j], dev(y=ring(y, d), zh=(zh + e) % 2))
     exp_pass(2)
+
+    settle(early + 12)
 
     for d, e in others[::-1]:
         got("td", d * 2 + e - 1, td.at[ring(y, -d) * 2 + (zh + e) % 2])
@@ -461,6 +491,8 @@
             def _():
                 dst[...] = src[...]
 
+    early = len(pending)
+    settle(early - 10)
     for d in (1, 3, 2):
         got("gq", d - 1, gqr.at[d - 1])
     radial(0, gqs[0] + gqr[0] + gqr[1] + gqr[2])
@@ -477,6 +509,7 @@
     hop(1, 0)
     columns(1, 1, 0)
     columns(1, 3, 0)
+    settle(early)
     near(0, 1)
     columns(0, 0, 1)
     columns(0, 2, 0)
@@ -537,30 +570,35 @@
         jnp.log(v[:, 0:64]) - v[:, 64:128] for v in (td[x * 2][0:1], td[x * 2 + 1][0:1])
     ]
     loss_ref[...] = jnp.concatenate(losses, axis=1)
+    settle(len(pending))
+    for n in range(32):
+        d, _, _, remote = column_copy(n // 16, n // 4 % 4, n // 2 % 2, n % 2)
+
+        @pl.when(d > 0)
+        def _():
+            remote.wait_send()
+
     for d in (1, 3, 2):
         got("wz", d - 1, wzr.at[d - 1])
     wg_ref[...] += wzr[0].astype(F32) + wzr[1].astype(F32) + wzr[2].astype(F32)
-    for c in pending:
-        c.wait_send()
     for d in (1, 2, 3):
         copy("wz", d - 1, wzs.at[d - 1], wzr.at[d - 1], dev(core=1 - core)).wait_send()
-    for n in range(32):
-        d, _, _, remote = column_copy(n // 16, n // 4 % 4, n // 2 % 2, n % 2)
-
-        @pl.when(d > 0)
-        def _():
-            remote.wait_send()
 
 
 def hand_over(*refs):
-    for k in range(4):
-        refs[4 + k][...] = refs[k][...]
+    copies = [pltpu.make_async_copy(refs[k], refs[4 + k], refs[8].at[k]) for k in range(4)]
+    for c in copies:
+        c.start()
+    for c in copies:
+        c.wait()
 
 
 def body(attn_out, residual, o_weight, norm_gain, positive):
     vmem = pl.BlockSpec(memory_space=pltpu.VMEM)
     shape = jax.ShapeDtypeStruct
     scratch = [
+        ((256, 512), BF16), ((256, 512), BF16), ((512, 4096), BF16), ((1, 512), F32),
+        ((1, 128), jnp.int32),
         ((4, 3, 128, 512), WIRE), ((4, 2, 64, 512), F32), ((4, 2, 64, 512), WIRE),
         ((4, 2, 128, 512), WIRE), ((4, 128, 512), F32),
         ((2, 128, 512), WIRE), ((2, 128, 512), WIRE), ((256, 512), F32), ((256, 128), F32),
@@ -583,13 +621,13 @@
     made = pl.pallas_call(
         kernel,
         name="step",
-        out_shape=outs,
-        in_specs=[vmem] * 5,
+        out_shape=tuple(pltpu.VMEM(v.shape, v.dtype) for v in outs),
+        in_specs=[pl.BlockSpec(memory_space=pl.ANY)] * 5,
         out_specs=[vmem] * 4,
         scratch_shapes=[pltpu.VMEM(s, t) for s, t in scratch]
-        + [pltpu.SemaphoreType.DMA((COUNT,)), pltpu.SemaphoreType.DMA((COUNT,))],
+        + [pltpu.SemaphoreType.DMA((n,)) for n in (COUNT, COUNT, 8)],
         compiler_params=pltpu.CompilerParams(
-            collective_id=0, has_side_effects=True, vmem_limit_bytes=40 * 1024 * 1024
+            collective_id=0, has_side_effects=True, vmem_limit_bytes=56 * 1024 * 1024
         ),
     )(
         attn_out.reshape(256, 512), residual.reshape(256, 512), o_weight,
@@ -600,7 +638,8 @@
         name="hand_over",
         out_shape=outs,
         in_specs=[vmem] * 4,
-        out_specs=[vmem] * 4,
+        out_specs=[pl.BlockSpec(memory_space=pl.ANY)] * 4,
+        scratch_shapes=[pltpu.SemaphoreType.DMA((4,))],
     )(*made)
     return (
         loss.reshape(128), rg.reshape(2, 128, 512), ag.reshape(2, 128, 512), wg,

time: 171 us -> 166 us (0.971)
  local copies, waits for them, and re-layouts: 8.26 us -> 2.74 us
    unnamed x18 -> x8, local copies, waits for them, and re-layouts: 8.26 us -> 2.74 us
where the time goes in v4:
time: 166 us; the launch traced here: 165 us
  Pallas kernels  162 us (98%)
  local copies, waits for them, and re-layouts  2.74 us (2%)
    pallas_call x1, Pallas kernels, body(): pl.pallas_call(kernel, name='step', out_shape=tuple((pltpu.VMEM(v.shape,...  160 us

profile of v4, /device:TPU:63, one launch (start us, length us, event | category | flops | bytes accessed | tf_op | source)
XLA Modules:
  0.0 165.4 jit_solution(10790335292641539587)
XLA Ops:
  0.6 159.6 %step.1 = (f32[1,128]{1,0:T(1,128)S(1)}, f32[256,512]{1,0:T(8,128)S(1)}, f32[256,512]{1,0:T(8,128)S(1)}, f32[512,128]{1,0:T(8,128)S(1)}) custom-call(bf16[256,512]{1,0:T(8,128)(2,1)} %bitcast.7, bf16[256,512]{1,0:T(8,128)(2,1)} %bitcast.8, bf16[512,4096]{1,0:T(8,128)(2,1)} %w_in.1, f32[1,512]{1,0:T(1,128)} %bitcast.9, s32[1,128]{1,0:T(1,128)} %bitcast.10), custom_call_target="tpu_custom_call" | custom-call | tf_op jit(solution)/shard_map/step/pallas_call | solution.py:621
  160.3 0.0 copy-start
  160.3 0.8 copy-done
  161.0 0.0 copy-start.1
  161.0 0.8 copy-done.1
  161.8 0.0 copy-start.2
  161.8 0.7 copy-done.2
  162.5 0.0 copy-start.3
  162.5 0.5 copy-done.3
  163.0 2.4 %hand_over.1 = (f32[1,128]{1,0:T(1,128)}, f32[256,512]{1,0:T(8,128)}, f32[256,512]{1,0:T(8,128)}, f32[512,128]{1,0:T(8,128)}) custom-call(f32[1,128]{1,0:T(1,128)} %copy-done.3, f32[256,512]{1,0:T(8,128)} %copy-done, f32[256,512]{1,0:T(8,128)} %copy-done.1, f32[512,128]{1,0:T(8,128)} %copy-done.2), custom_call_target="tpu_custom_call" | custom-call | tf_op jit(solution)/shard_map/hand_over/pallas_call | solution.py:636
Async XLA Ops:
  160.3 0.8 copy-start
  161.0 0.8 copy-start.1
  161.8 0.7 copy-start.2
  162.5 0.5 copy-start.3

commit v5 on v4

--- a/solution.py
+++ b/solution.py
@@ -640,6 +640,7 @@
         in_specs=[vmem] * 4,
         out_specs=[pl.BlockSpec(memory_space=pl.ANY)] * 4,
         scratch_shapes=[pltpu.SemaphoreType.DMA((4,))],
+        compiler_params=pltpu.CompilerParams(vmem_limit_bytes=4 * 1024 * 1024),
     )(*made)
     return (
         loss.reshape(128), rg.reshape(2, 128, 512), ag.reshape(2, 128, 512), wg,

time: 166 us -> 162 us (0.976)
  local copies, waits for them, and re-layouts: 2.74 us -> 0 us
    unnamed x8 -> x0, local copies, waits for them, and re-layouts: 2.74 us -> none
where the time goes in v5:
time: 162 us; the launch traced here: 161 us
  Pallas kernels  161 us (99%)
    pallas_call x1, Pallas kernels, body(): pl.pallas_call(kernel, name='step', out_shape=tuple((pltpu.VMEM(v.shape,...  160 us

profile of v5, /device:TPU:63, one launch (start us, length us, event | category | flops | bytes accessed | tf_op | source)
XLA Modules:
  0.0 161.3 jit_solution(4909758771027615254)
XLA Ops:
  0.6 159.6 %step.1 = (f32[1,128]{1,0:T(1,128)S(1)}, f32[256,512]{1,0:T(8,128)S(1)}, f32[256,512]{1,0:T(8,128)S(1)}, f32[512,128]{1,0:T(8,128)S(1)}) custom-call(bf16[256,512]{1,0:T(8,128)(2,1)} %bitcast.7, bf16[256,512]{1,0:T(8,128)(2,1)} %bitcast.8, bf16[512,4096]{1,0:T(8,128)(2,1)} %w_in.1, f32[1,512]{1,0:T(1,128)} %bitcast.9, s32[1,128]{1,0:T(1,128)} %bitcast.10), custom_call_target="tpu_custom_call" | custom-call | tf_op jit(solution)/shard_map/step/pallas_call | solution.py:621
  160.3 1.1 hand_over.1

commit v6 on v5

--- a/solution.py
+++ b/solution.py
@@ -188,10 +188,10 @@
         return (sc[half(h), :] * inv).astype(BF16)
 
     y_products(0)
-    y_products(1)
     px[x] = jnp.broadcast_to(pos_ref[...], (8, 128))
     pl.semaphore_wait(barrier, len(peers))
     y_send(0)
+    y_products(1)
     y_send(2)
     for d in (2, 1, 3):
         go("ps", d - 1, px.at[x], px.at[x], dev(x=ring(x, d)))
@@ -365,7 +365,7 @@
         at = pl.ds(xx * 128, 128)
         pos_s[0, at, :] = jnp.broadcast_to(to_col(scale), (128, 128))
         pos_s[1, at, :] = jnp.broadcast_to(
-            to_col(jnp.exp(top) * scale - LOGIT_SCALE), (128, 128)
+            to_col(-LOGIT_SCALE * ((total - jnp.exp(top)) / total)), (128, 128)
         )
 
     def score(t):
@@ -457,6 +457,11 @@
                 got("gh", h * 2 + c, part)
             go("gy", h * 12 + k * 6 + c, part, part, right)
             go("gy", h * 12 + k * 6 + 2 + c, part, part, left)
+            if straight(h, k):
+                go("gy", h * 12 + k * 6 + 4 + c, part, part, dev(y=ring(y, 2)))
+
+    def straight(h, k):
+        return h == 1 and k == 1
 
     def hop(h, k):
         e = zh if k == 0 else 1 - zh
@@ -477,7 +482,10 @@
         return d, src, dst, copy("gx", (n * 2 + k) * 2 + c, src, dst, dev(x=xx), n * 3 + d - 1)
 
     def columns(h, t, k):
-        for n, c in {0: (), 1: ((1, 1),), 3: ((2, 0),), 2: ((4, 0), (5, 1))}[t]:
+        arrivals = {0: (), 1: ((1, 1),), 3: ((2, 0),), 2: ((4, 0), (5, 1))}[t]
+        if straight(h, k):
+            arrivals += {0: (), 1: ((0, 0),), 3: ((3, 1),), 2: ()}[t]
+        for n, c in arrivals:
             e = zh if k == 0 else 1 - zh
             got("gy", h * 12 + k * 6 + n, gg.at[ring(y, -t) * 2 + e, c, half(h)])
         for c in (0, 1):
@@ -520,7 +528,6 @@
     near(1, 1)
     columns(1, 0, 1)
     columns(0, 2, 1)
-    hop(1, 1)
 
     for d in (1, 3, 2):
         got("ax", d - 1, ax.at[rows(ring(x, -d) * 256, 256)])
@@ -560,15 +567,21 @@
     weight_sum(1)
     weight_sum(3)
 
+    weight_part(2)
+    weight_sum(2)
     ag_ref[...] = jnp.zeros((256, 512), F32)
     for jj in range(8):
         for c in (0, 1):
             ag_ref[...] += nt(gg[jj, c], w_ref[:, pl.ds(jj * 512 + c * 256, 256)])
-    weight_part(2)
-    weight_sum(2)
-    losses = [
-        jnp.log(v[:, 0:64]) - v[:, 64:128] for v in (td[x * 2][0:1], td[x * 2 + 1][0:1])
-    ]
+    losses = []
+    for v in (td[x * 2][0:1], td[x * 2 + 1][0:1]):
+        total, top = v[:, 0:64], v[:, 64:128]
+        peak = jnp.exp(top)
+        losses.append(
+            jnp.where(
+                total < 4.0 * peak, jnp.log1p((total - peak) / peak), jnp.log(total) - top
+            )
+        )
     loss_ref[...] = jnp.concatenate(losses, axis=1)
     settle(len(pending))
     for n in range(32):

time: 162 us -> 160 us (0.988)
  Pallas kernels: 161 us -> 158 us
    pallas_call x1, Pallas kernels: 160 us -> 157 us  [body(): pl.pallas_call(kernel, name='step', out_shape=tuple((pltpu.VMEM(v.shape,...]
where the time goes in v6:
time: 160 us; the launch traced here: 159 us
  Pallas kernels  158 us (99%)
    pallas_call x1, Pallas kernels, body(): pl.pallas_call(kernel, name='step', out_shape=tuple((pltpu.VMEM(v.shape,...  157 us

profile of v6, /device:TPU:63, one launch (start us, length us, event | category | flops | bytes accessed | tf_op | source)
XLA Modules:
  0.0 159.0 jit_solution(10944879180748841512)
XLA Ops:
  0.6 157.3 %step.1 = (f32[1,128]{1,0:T(1,128)S(1)}, f32[256,512]{1,0:T(8,128)S(1)}, f32[256,512]{1,0:T(8,128)S(1)}, f32[512,128]{1,0:T(8,128)S(1)}) custom-call(bf16[256,512]{1,0:T(8,128)(2,1)} %bitcast.7, bf16[256,512]{1,0:T(8,128)(2,1)} %bitcast.8, bf16[512,4096]{1,0:T(8,128)(2,1)} %w_in.1, f32[1,512]{1,0:T(1,128)} %bitcast.9, s32[1,128]{1,0:T(1,128)} %bitcast.10), custom_call_target="tpu_custom_call" | custom-call | tf_op jit(solution)/shard_map/step/pallas_call | solution.py:634
  157.9 1.1 hand_over.1

commit v7 on v6

--- a/solution.py
+++ b/solution.py
@@ -10,7 +10,7 @@
 F32 = jnp.float32
 BF16 = jnp.bfloat16
 MESH = pl.DeviceIdType.MESH
-WIRE = BF16
+WIRE = F32
 GZ_WIRE = BF16
 WZ_WIRE = BF16
 

time: 160 us -> 180 us (1.12)
  Pallas kernels: 158 us -> 180 us
    pallas_call x1, Pallas kernels: 157 us -> 179 us  [body(): pl.pallas_call(kernel, name='step', out_shape=tuple((pltpu.VMEM(v.shape,...]
where the time goes in v7:
time: 180 us
  Pallas kernels  180 us (100%)
    pallas_call x1, Pallas kernels, body(): pl.pallas_call(kernel, name='step', out_shape=tuple((pltpu.VMEM(v.shape,...  179 us

profile of v7, /device:TPU:63, one launch (start us, length us, event | category | flops | bytes accessed | tf_op | source)
XLA Modules:
  0.0 180.2 jit_solution(2803990333439670396)
XLA Ops:
  0.6 178.5 %step.1 = (f32[1,128]{1,0:T(1,128)S(1)}, f32[256,512]{1,0:T(8,128)S(1)}, f32[256,512]{1,0:T(8,128)S(1)}, f32[512,128]{1,0:T(8,128)S(1)}) custom-call(bf16[256,512]{1,0:T(8,128)(2,1)} %bitcast.7, bf16[256,512]{1,0:T(8,128)(2,1)} %bitcast.8, bf16[512,4096]{1,0:T(8,128)(2,1)} %w_in.1, f32[1,512]{1,0:T(1,128)} %bitcast.9, s32[1,128]{1,0:T(1,128)} %bitcast.10), custom_call_target="tpu_custom_call" | custom-call | tf_op jit(solution)/shard_map/step/pallas_call | solution.py:634
  179.1 1.1 hand_over.1

commit v8 on v6

--- a/solution.py
+++ b/solution.py
@@ -128,7 +128,7 @@
         return nn(a_ref[half(h), :], w_ref[:, rows(yy * 1024 + e * 512, 512)])
 
     low, high = pl.ds(0, 64), pl.ds(64, 64)
-    right, left = dev(y=ring(y, 1)), dev(y=ring(y, 3))
+    right, left, opposite = dev(y=ring(y, 1)), dev(y=ring(y, 3)), dev(y=ring(y, 2))
 
     def y_products(h):
         for er in (0, 1):
@@ -253,8 +253,12 @@
         for er in (0, 1):
             k = t * 12 + er * 6
             far, after, before = (logit_piece(t, er, d) for d in (2, 1, 3))
-            go("ly", k + 0, far.at[top], lt.at[t, er, 0], right)
-            go("ly", k + 1, far.at[end], lt.at[t, er, 1], left)
+            last = t == 2
+            go("ly", k + 0, far.at[top], lt.at[t, er, 0], opposite if last else right)
+            go("ly", k + 1, far.at[end], lt.at[t, er, 1], opposite if last else left)
+            if last:
+                go("ly", k + 4, after.at[top], lr.at[t, er, 0, top], right)
+                go("ly", k + 5, before.at[end], lr.at[t, er, 1, end], left)
             go("ly", k + 2, after.at[end], lr.at[t, er, 0, end], right)
             go("ly", k + 3, before.at[top], lr.at[t, er, 1, top], left)
 
@@ -280,7 +284,12 @@
         got("ly", k + 3, lr.at[t, er, 1, top])
         got("ly", k + 4, lr.at[t, er, 0, top])
         got("ly", k + 5, lr.at[t, er, 1, end])
-        return lg[t, pair if er == 0 else mine, :] + lr[t, er, 0] + lr[t, er, 1]
+        part = lg[t, pair if er == 0 else mine, :] + lr[t, er, 0] + lr[t, er, 1]
+        if t == 2:
+            got("ly", k + 0, lt.at[t, er, 0])
+            got("ly", k + 1, lt.at[t, er, 1])
+            part = part + jnp.concatenate([lt[t, er, 0], lt[t, er, 1]], axis=0)
+        return part
 
     def logit_pass(t):
         lzs[t] = logit_sum(t, 0)
@@ -329,7 +338,6 @@
     logit_pass(0)
     logit_hop(3)
     logit_pass(1)
-    logit_hop(2)
     settle(early)
     logit_done(0)
     logit_pass(3)

time: 160 us -> 160 us (level)
  Pallas kernels: 158 us -> 160 us
where the time goes in v8:
time: 160 us
  Pallas kernels  160 us (100%)
    pallas_call x1, Pallas kernels, body(): pl.pallas_call(kernel, name='step', out_shape=tuple((pltpu.VMEM(v.shape,...  159 us

profile of v8, /device:TPU:63, one launch (start us, length us, event | category | flops | bytes accessed | tf_op | source)
XLA Modules:
  0.0 160.4 jit_solution(848350827195096604)
XLA Ops:
  0.6 158.7 %step.1 = (f32[1,128]{1,0:T(1,128)S(1)}, f32[256,512]{1,0:T(8,128)S(1)}, f32[256,512]{1,0:T(8,128)S(1)}, f32[512,128]{1,0:T(8,128)S(1)}) custom-call(bf16[256,512]{1,0:T(8,128)(2,1)} %bitcast.7, bf16[256,512]{1,0:T(8,128)(2,1)} %bitcast.8, bf16[512,4096]{1,0:T(8,128)(2,1)} %w_in.1, f32[1,512]{1,0:T(1,128)} %bitcast.9, s32[1,128]{1,0:T(1,128)} %bitcast.10), custom_call_target="tpu_custom_call" | custom-call | tf_op jit(solution)/shard_map/step/pallas_call | solution.py:642
  159.3 1.1 hand_over.1

commit v9 on v8

--- a/solution.py
+++ b/solution.py
@@ -309,7 +309,8 @@
         ex = jnp.exp(logits)
         ea[t, mine, :] = ex.astype(BF16)
         go("ez", t, ea.at[t, mine], ea.at[t, mine], dev(zh=1 - zh))
-        exp_send(t, zh)
+        if t != 2:
+            exp_send(t, zh)
         hit = jnp.concatenate([hits(t, mine, 0), hits(t, mine, 1)], axis=1)
         sums_s[t] = jnp.concatenate(
             [
@@ -353,6 +354,7 @@
     txb[0] = to_row(sums_s[0] + sums_s[1] + sums_s[2] + sums_s[3])
     for d in (2, 1, 3):
         go("tx", d - 1, txb.at[0], txb.at[d], dev(x=ring(x, d)))
+    exp_send(2, zh)
     exp_pass(3)
     for d in (1, 3, 2):
         got("tx", d - 1, txb.at[d])
@@ -449,13 +451,13 @@
         rad = to_col(tot[0:1])
         iv = inv_s[at, 0:1]
         out = gain_ref[...] * (iv * ge[at, :] - (iv * iv * iv * rad) * sc[at, :])
-        rg_ref[at, :] = out
         for c in (0, 1):
             gg[j, c, at, :] = out[:, c * 256:(c + 1) * 256].astype(BF16)
         for c in (0, 1):
             part = gg.at[j, c, at]
             go("gh", h * 2 + c, part, part, dev(zh=1 - zh))
         near(h, 0)
+        rg_ref[at, :] = out
 
     def near(h, k):
         e = zh if k == 0 else 1 - zh

time: 160 us -> 160 us (level)
  no operation moved by 1% of the time
where the time goes in v9:
time: 160 us
  Pallas kernels  160 us (100%)
    pallas_call x1, Pallas kernels, body(): pl.pallas_call(kernel, name='step', out_shape=tuple((pltpu.VMEM(v.shape,...  159 us

profile of v9, /device:TPU:63, one launch (start us, length us, event | category | flops | bytes accessed | tf_op | source)
XLA Modules:
  0.0 160.4 jit_solution(11893909299886197520)
XLA Ops:
  0.6 158.7 %step.1 = (f32[1,128]{1,0:T(1,128)S(1)}, f32[256,512]{1,0:T(8,128)S(1)}, f32[256,512]{1,0:T(8,128)S(1)}, f32[512,128]{1,0:T(8,128)S(1)}) custom-call(bf16[256,512]{1,0:T(8,128)(2,1)} %bitcast.7, bf16[256,512]{1,0:T(8,128)(2,1)} %bitcast.8, bf16[512,4096]{1,0:T(8,128)(2,1)} %w_in.1, f32[1,512]{1,0:T(1,128)} %bitcast.9, s32[1,128]{1,0:T(1,128)} %bitcast.10), custom_call_target="tpu_custom_call" | custom-call | tf_op jit(solution)/shard_map/step/pallas_call | solution.py:644
  159.3 1.1 hand_over.1
